TPU v7x, 128 devices: a whole 4x4x4 slice. The times are simulated.
128 devices in a mesh: tm: 32 (over y, x, core), gz: 4 (over z).
Axes of the slice: x: 4, y: 4, z: 4, core: 2. Of those that a mesh axis runs over, the one named last changes fastest.
Arguments:
- state_rhs: float32 [128, 128, 2048], P('tm', 'gz'), may hold values from -6 to 6
- adjoint_rhs: float32 [128, 128, 2048], P('tm', 'gz'), may hold values from -6 to 6
- diffusivity: float32 [128, 2048], P('gz'), may hold values from 0.02 to 2
- velocity: float32 [3, 128, 2048], P(None, 'gz'), may hold values from -4 to 4
Outputs:
- state_out: float32 [128, 128, 2048], P('tm', 'gz')
- adjoint_out: float32 [128, 128, 2048], P('tm', 'gz')
All inputs are finite; a program needn't handle non-finite values.
Results may differ from a plain program's by a relative error of at most 0.0003.
Values sent between devices are 32-bit elements; how exact they have to be, the bound alone decides.
A program may use at most 128 MiB of HBM per device.

v0:
```python
import math

import jax
import jax.numpy as jnp
from jax import lax
from jax.sharding import PartitionSpec as P

NY = 64


alpha_wrap = 0.1
beta_couple = 0.5
gamma_couple = 0.5


def padded(cells, sides, width):
    for axis, dim in sides:
        count = lax.axis_size(axis)
        ends = count - 1
        head = lax.slice_in_dim(cells, 0, width, axis=dim)
        tail = lax.slice_in_dim(cells, cells.shape[dim] - width, cells.shape[dim], axis=dim)
        cells = jnp.concatenate(
            [
                lax.ppermute(tail, axis, [(i, (i + 1) % count) for i in range(ends)]),
                cells,
                lax.ppermute(head, axis, [((i + 1) % count, i) for i in range(ends)]),
            ],
            axis=dim,
        )
    return cells


def swapped(value, axis, bit):
    mask = 2**bit
    pairs = [(source, source ^ mask) for source in range(lax.axis_size(axis))]
    return lax.ppermute(value, axis, pairs)


def ahead_flat(field, stride):
    pad_shape = field.shape[:-1] + (stride,)
    return jnp.concatenate([field[..., stride:], jnp.zeros(pad_shape, field.dtype)], axis=-1)


def behind_flat(field, stride):
    pad_shape = field.shape[:-1] + (stride,)
    return jnp.concatenate([jnp.zeros(pad_shape, field.dtype), field[..., :-stride]], axis=-1)


def neighbour_pairs(field, field_pad, width_y):
    column = jnp.arange(field.shape[-1], dtype=jnp.int32) % width_y
    nothing = jnp.zeros((), field.dtype)
    y_ahead = jnp.where(column == width_y - 1, nothing, ahead_flat(field, 1))
    y_behind = jnp.where(column == 0, nothing, behind_flat(field, 1))
    return [
        (field_pad[..., 2:, :], field_pad[..., :-2, :]),
        (ahead_flat(field, width_y), behind_flat(field, width_y)),
        (y_ahead, y_behind),
    ]


def face_weights(kappa, kappa_pad, width_y):
    pairs = neighbour_pairs(kappa, kappa_pad, width_y)
    weights = []
    diagonal = jnp.zeros_like(kappa)
    for ahead, behind in pairs:
        face_ahead = jnp.where(ahead > 0.0, 0.5 * (kappa + ahead), kappa)
        face_behind = jnp.where(behind > 0.0, 0.5 * (kappa + behind), kappa)
        weights.append((face_ahead, face_behind))
        diagonal = diagonal + face_ahead + face_behind
    return (weights, diagonal)


def coupling(field, field_pad, weights, velocity, width_y):
    sign = jnp.array([1.0, -1.0, 1.0, -1.0], field.dtype).reshape((4,) + (1,) * (field.ndim - 1))
    pairs = neighbour_pairs(field, field_pad, width_y)
    speeds = [velocity[2], velocity[0], velocity[1]]
    total = jnp.zeros_like(field)
    for index in range(3):
        ahead, behind = pairs[index]
        face_ahead, face_behind = weights[index]
        total = (
            total
            + face_ahead * ahead
            + face_behind * behind
            - sign * (0.5 * speeds[index]) * (ahead - behind)
        )
    return total


def apply_split(stacked, lam_real, lam_real_other, lam_imag, diagonal):
    shifted = lam_real + diagonal
    shifted_other = lam_real_other + diagonal
    determinant = shifted * shifted + lam_imag * lam_imag + beta_couple * gamma_couple
    determinant_other = (
        shifted_other * shifted_other + lam_imag * lam_imag + beta_couple * gamma_couple
    )
    state_real, adjoint_real, state_imag, adjoint_imag = (
        stacked[0],
        stacked[1],
        stacked[2],
        stacked[3],
    )
    out_state_real = (
        shifted * state_real + lam_imag * state_imag + beta_couple * adjoint_real
    ) / determinant
    out_state_imag = (
        shifted_other * state_imag - lam_imag * state_real + beta_couple * adjoint_imag
    ) / determinant_other
    out_adjoint_real = (
        shifted * adjoint_real - lam_imag * adjoint_imag - gamma_couple * state_real
    ) / determinant
    out_adjoint_imag = (
        shifted_other * adjoint_imag + lam_imag * adjoint_real - gamma_couple * state_imag
    ) / determinant_other
    return jnp.stack([out_state_real, out_adjoint_real, out_state_imag, out_adjoint_imag])


def mix_rows(matrix, data):
    return jnp.einsum("ab,sbm->sam", matrix, data, precision=lax.Precision.HIGHEST)


def body(state_rhs, adjoint_rhs, diffusivity, velocity):
    steps_local, depth, cells = state_rhs.shape
    ranks = lax.axis_size("tm")
    rank = lax.axis_index("tm")
    total = steps_local * ranks
    two_pi = 2.0 * math.pi
    ratio = alpha_wrap ** (1.0 / total)
    kappa_pad = padded(diffusivity, (("gz", 0),), 1)
    weights, diagonal = face_weights(diffusivity, kappa_pad, NY)
    fields = jnp.stack([state_rhs, adjoint_rhs])
    local_steps = jnp.arange(steps_local, dtype=jnp.int32)
    bits = ranks.bit_length() - 1
    times_here = rank * steps_local + local_steps
    damping = jnp.power(jnp.float32(alpha_wrap), times_here.astype(jnp.float32) / total)
    scaled = fields * damping[None, :, None, None]
    top = bits - 1
    partner = swapped(scaled, "tm", top)
    high = rank >> top & 1 == 1
    position = (rank & (1 << top) - 1).astype(jnp.float32)
    cosine = jnp.cos(math.pi * position / (1 << top))
    sine = jnp.sin(math.pi * position / (1 << top))
    spread = partner - scaled
    real_part = jnp.where(high, spread * cosine, scaled + partner)
    imag_part = jnp.where(high, -spread * sine, jnp.zeros_like(spread))
    data = jnp.concatenate([real_part, imag_part])
    for level in range(1, bits):
        bit = bits - 1 - level
        half = 1 << bit
        partner = swapped(data, "tm", bit)
        high = rank >> bit & 1 == 1
        position = (rank & half - 1).astype(jnp.float32)
        cosine = jnp.cos(math.pi * position / half)
        sine = jnp.sin(math.pi * position / half)
        spread = partner - data
        turned = jnp.concatenate(
            [spread[:2] * cosine + spread[2:] * sine, spread[2:] * cosine - spread[:2] * sine]
        )
        data = jnp.where(high, turned, data + partner)
    reversed_rank = jnp.zeros((), jnp.int32)
    for bit in range(bits):
        reversed_rank = reversed_rank + ((rank >> bit & 1) << bits - 1 - bit)
    frequency = reversed_rank + ranks * local_steps
    phase = (frequency[:, None] * local_steps[None, :] % total).astype(jnp.float32) * (
        two_pi / total
    )
    grid_real = jnp.cos(phase)
    grid_imag = -jnp.sin(phase)
    flat = data.reshape(4, steps_local, depth * cells)
    out_real = mix_rows(grid_real, flat[:2]) - mix_rows(grid_imag, flat[2:])
    out_imag = mix_rows(grid_real, flat[2:]) + mix_rows(grid_imag, flat[:2])
    blocks = jnp.concatenate([out_real, out_imag]).reshape(4, steps_local, depth, cells)
    angle = (frequency % total).astype(jnp.float32) * (two_pi / total)
    lam_real = (1.0 - ratio * jnp.cos(angle)).reshape(steps_local, 1, 1)
    lam_imag = (ratio * jnp.sin(angle)).reshape(steps_local, 1, 1)
    first = apply_split(blocks, lam_real, lam_real, lam_imag, diagonal)
    first_pad = padded(first, (("gz", 2),), 1)
    solved = apply_split(
        blocks + coupling(first, first_pad, weights, velocity, NY),
        lam_real,
        lam_real,
        lam_imag,
        diagonal,
    )
    phase = (local_steps[:, None] * frequency[None, :] % total).astype(jnp.float32) * (
        two_pi / total
    )
    grid_real = jnp.cos(phase)
    grid_imag = jnp.sin(phase)
    flat = solved.reshape(4, steps_local, depth * cells)
    back_real = mix_rows(grid_real, flat[:2]) - mix_rows(grid_imag, flat[2:])
    back_imag = mix_rows(grid_real, flat[2:]) + mix_rows(grid_imag, flat[:2])
    data = jnp.concatenate([back_real, back_imag]).reshape(4, steps_local, depth, cells)
    for bit in range(bits):
        half = 1 << bit
        partner = swapped(data, "tm", bit)
        high = rank >> bit & 1 == 1
        position = (rank & half - 1).astype(jnp.float32)
        cosine = jnp.cos(math.pi * position / half)
        sine = jnp.sin(math.pi * position / half)
        other = jnp.where(high, data, partner)
        base = jnp.where(high, partner, data)
        turned = jnp.concatenate(
            [other[:2] * cosine - other[2:] * sine, other[:2] * sine + other[2:] * cosine]
        )
        data = jnp.where(high, base - turned, base + turned)
    undo = jnp.power(jnp.float32(alpha_wrap), -times_here.astype(jnp.float32) / total) / total
    result = data[:2] * undo[None, :, None, None]
    return (result[0], result[1])


def solution(mesh):
    placed = (P("tm", "gz", None), P("tm", "gz", None), P("gz", None), P(None, "gz", None))
    return jax.shard_map(
        body,
        mesh=mesh,
        in_specs=placed,
        out_specs=(P("tm", "gz", None), P("tm", "gz", None)),
        check_vma=False,
    )
```

profile of v0, /device:TPU:1, one launch (start us, length us, event | category | flops | bytes accessed | tf_op | source)
XLA Modules:
  0.0 890.4 jit_solution(3531315405878219138)
XLA Ops:
  2.6 3.8 collective-permute-start.2
  6.6 45.0 %collective-permute-done.2 = f32[2,4,32,2048]{3,2,1,0:T(8,128)} collective-permute-done((f32[2,4,32,2048]{3,2,1,0:T(8,128)S(1)}, f32[2,4,32,2048]{3,2,1,0:T(8,128)}, u32[]{:S(2)}, u32[]{:S(2)}) %collective-permute-start.2) | collective-permute-done | bytes 2097184 | tf_op jit(solution)/shard_map/ppermute | solution.py:36
  58.2 89.4 %collective-permute-done.3 = f32[4,4,32,2048]{3,2,1,0:T(8,128)} collective-permute-done((f32[4,4,32,2048]{3,2,1,0:T(8,128)}, f32[4,4,32,2048]{3,2,1,0:T(8,128)}, u32[]{:S(2)}, u32[]{:S(2)}) %collective-permute-start.3) | collective-permute-done | bytes 4194336 | tf_op jit(solution)/shard_map/ppermute | solution.py:36
  152.8 5.5 maximum_select_fusion
  161.2 88.6 %collective-permute-done.4 = f32[4,4,32,2048]{3,2,1,0:T(8,128)} collective-permute-done((f32[4,4,32,2048]{3,2,1,0:T(8,128)}, f32[4,4,32,2048]{3,2,1,0:T(8,128)}, u32[]{:S(2)}, u32[]{:S(2)}) %collective-permute-start.4) | collective-permute-done | bytes 4194336 | tf_op jit(solution)/shard_map/ppermute | solution.py:36
  249.8 4.2 sub.154
  254.6 6.8 maximum_select_fusion.1
  262.7 87.7 %collective-permute-done.5 = f32[4,4,32,2048]{3,2,1,0:T(8,128)} collective-permute-done((f32[4,4,32,2048]{3,2,1,0:T(8,128)}, f32[4,4,32,2048]{3,2,1,0:T(8,128)}, u32[]{:S(2)}, u32[]{:S(2)}) %collective-permute-start.5) | collective-permute-done | bytes 4194336 | tf_op jit(solution)/shard_map/ppermute | solution.py:36
  350.4 4.2 sub.156
  355.3 6.8 maximum_select_fusion.2
  362.1 4.3 collective-permute-start.6
  376.0 4.2 sub.158
  380.6 4.8 maximum_select_fusion.3
  390.4 3.7 slice.219
  394.1 4.0 fusion.55
  398.1 4.0 fusion.57
  402.1 4.2 fusion.2
  406.3 4.6 fusion.3
  418.9 4.9 fusion.112
  428.6 4.8 fusion.111
  433.4 6.2 reshape.290
  439.6 12.3 %subtract_add_fusion = f32[4,4,32,2048]{3,2,1,0:T(8,128)S(1)} fusion(f32[4,4,32,2048]{3,2,1,0:T(8,128)} %reshape.290, f32[4,4,32,2047]{3,2,1,0:T(8,128)} %get-tuple-element.28, f32[4,4,32,2047]{3,2,1,0:T(8,128)} %get-tuple-element.27, f32[4,4,32,1984]{3,2,1,0:T(8,128)} %get-tuple-element.26, f32[4,4,32,1984]{3,2,1,0:T(8,128)} %get-tuple-element.25, ...), kind=kLoop, calls=%fused_computation.41 | loop fusion | flops 32505856 | bytes 34078720 | tf_op jit(solution)/shard_map/add | solution.py:179
  458.3 4.9 fusion.51
  468.3 5.5 fusion.53
  473.8 4.3 fusion
  478.1 4.1 fusion.1
  485.1 6.1 reshape.291
  493.0 7.0 collective-permute-done.9
  508.3 89.7 %collective-permute-done.10 = f32[4,4,32,2048]{3,2,1,0:T(8,128)S(1)} collective-permute-done((f32[4,4,32,2048]{3,2,1,0:T(8,128)S(1)}, f32[4,4,32,2048]{3,2,1,0:T(8,128)S(1)}, u32[]{:S(2)}, u32[]{:S(2)}) %collective-permute-start.10) | collective-permute-done | bytes 4194336 | tf_op jit(solution)/shard_map/ppermute | solution.py:36
  604.9 90.8 %collective-permute-done.11 = f32[4,4,32,2048]{3,2,1,0:T(8,128)S(1)} collective-permute-done((f32[4,4,32,2048]{3,2,1,0:T(8,128)S(1)}, f32[4,4,32,2048]{3,2,1,0:T(8,128)S(1)}, u32[]{:S(2)}, u32[]{:S(2)}) %collective-permute-start.11) | collective-permute-done | bytes 4194336 | tf_op jit(solution)/shard_map/ppermute | solution.py:36
  700.3 90.5 %collective-permute-done.12 = f32[4,4,32,2048]{3,2,1,0:T(8,128)S(1)} collective-permute-done((f32[4,4,32,2048]{3,2,1,0:T(8,128)S(1)}, f32[4,4,32,2048]{3,2,1,0:T(8,128)S(1)}, u32[]{:S(2)}, u32[]{:S(2)}) %collective-permute-start.12) | collective-permute-done | bytes 4194336 | tf_op jit(solution)/shard_map/ppermute | solution.py:36
  796.9 89.4 %collective-permute-done.13 = f32[4,4,32,2048]{3,2,1,0:T(8,128)S(1)} collective-permute-done((f32[4,4,32,2048]{3,2,1,0:T(8,128)S(1)}, f32[4,4,32,2048]{3,2,1,0:T(8,128)S(1)}, u32[]{:S(2)}, u32[]{:S(2)}) %collective-permute-start.13) | collective-permute-done | bytes 4194336 | tf_op jit(solution)/shard_map/ppermute | solution.py:36
  (99 shorter events, 91.8 us)
Async XLA Ops:
  0.6 51.0 %copy-start.8 = (f32[4,32,2048]{2,1,0:T(8,128)S(1)}, f32[4,32,2048]{2,1,0:T(8,128)}, u32[]{:S(2)}) copy-start(f32[4,32,2048]{2,1,0:T(8,128)} %param.6) | copy-start | bytes 3145732
  2.6 49.0 %collective-permute-start.2 = (f32[2,4,32,2048]{3,2,1,0:T(8,128)S(1)}, f32[2,4,32,2048]{3,2,1,0:T(8,128)}, u32[]{:S(2)}, u32[]{:S(2)}) collective-permute-start(f32[2,4,32,2048]{3,2,1,0:T(8,128)S(1)} %maximum_multiply_fusion), channel_id=1, source_target_pairs={{0,64},{4,68},{8,72},{12,76},{16,80},{20,84},{24,88},{28,92},{32,9... | collective-permute-start | bytes 6291464 | tf_op jit(solution)/shard_map/ppermute | solution.py:36
  54.1 2.7 copy-start.1
  56.7 90.9 %collective-permute-start.3 = (f32[4,4,32,2048]{3,2,1,0:T(8,128)}, f32[4,4,32,2048]{3,2,1,0:T(8,128)}, u32[]{:S(2)}, u32[]{:S(2)}) collective-permute-start(f32[4,4,32,2048]{3,2,1,0:T(8,128)} %pad_maximum_fusion.8), channel_id=1, source_target_pairs={{0,32},{4,36},{8,40},{12,44},{16,48},{20,52},{24,56},{28,60},{32,0... | collective-permute-start | bytes 12582920 | tf_op jit(solution)/shard_map/ppermute | solution.py:36
  151.2 1.6 copy-start.2
  158.3 91.5 %collective-permute-start.4 = (f32[4,4,32,2048]{3,2,1,0:T(8,128)}, f32[4,4,32,2048]{3,2,1,0:T(8,128)}, u32[]{:S(2)}, u32[]{:S(2)}) collective-permute-start(f32[4,4,32,2048]{3,2,1,0:T(8,128)} %maximum_select_fusion), channel_id=1, source_target_pairs={{0,16},{4,20},{8,24},{12,28},{16,0},{20,4},{24,8},{28,12},{32,48},... | collective-permute-start | bytes 12582920 | tf_op jit(solution)/shard_map/ppermute | solution.py:36
  261.4 89.0 %collective-permute-start.5 = (f32[4,4,32,2048]{3,2,1,0:T(8,128)}, f32[4,4,32,2048]{3,2,1,0:T(8,128)}, u32[]{:S(2)}, u32[]{:S(2)}) collective-permute-start(f32[4,4,32,2048]{3,2,1,0:T(8,128)} %maximum_select_fusion.1), channel_id=1, source_target_pairs={{0,8},{4,12},{8,0},{12,4},{16,24},{20,28},{24,16},{28,20},{32,40},... | collective-permute-start | bytes 12582920 | tf_op jit(solution)/shard_map/ppermute | solution.py:36
  355.3 11.1 %copy-start.7 = (f32[32,2048]{1,0:T(8,128)S(1)}, f32[32,2048]{1,0:T(8,128)}, u32[]{:S(2)}) copy-start(f32[32,2048]{1,0:T(8,128)} %param.7) | copy-start | bytes 786436
  362.1 9.7 %copy-start.10 = (f32[3,32,2048]{2,1,0:T(8,128)S(1)}, f32[3,32,2048]{2,1,0:T(8,128)}, u32[]{:S(2)}) copy-start(f32[3,32,2048]{2,1,0:T(8,128)} %param.8) | copy-start | bytes 2359300
  362.1 9.8 %copy-start.15 = (f32[4]{0:T(128)S(1)}, f32[4]{0:T(128)}, u32[]{:S(2)}) copy-start(f32[4]{0:T(128)} %constant.115.clone) | copy-start | bytes 52
  362.1 13.9 %collective-permute-start.6 = (f32[4,4,32,2048]{3,2,1,0:T(8,128)}, f32[4,4,32,2048]{3,2,1,0:T(8,128)}, u32[]{:S(2)}, u32[]{:S(2)}) collective-permute-start(f32[4,4,32,2048]{3,2,1,0:T(8,128)} %maximum_select_fusion.2), channel_id=1, source_target_pairs={{0,4},{4,0},{8,12},{12,8},{16,20},{20,16},{24,28},{28,24},{32,36},... | collective-permute-start | bytes 12582920 | tf_op jit(solution)/shard_map/ppermute | solution.py:36
  366.4 7.4 collective-permute-start.1
  369.9 4.6 collective-permute-start
  371.5 42.6 %copy-start.11 = (f32[4]{0:T(128)}, f32[4]{0:T(128)S(1)}, u32[]{:S(2)}) copy-start(f32[4]{0:T(128)S(1)} %get-tuple-element.64) | copy-start | bytes 52
  373.7 40.4 %copy-start.13 = (f32[4]{0:T(128)}, f32[4]{0:T(128)S(1)}, u32[]{:S(2)}) copy-start(f32[4]{0:T(128)S(1)} %fusion.107) | copy-start | bytes 52
  394.1 4.0 copy-start.3
  417.0 1.0 copy-start.5
  423.8 15.8 %collective-permute-start.8 = (f32[4,4,1,2048]{3,2,1,0:T(1,128)}, f32[4,4,1,2048]{3,2,1,0:T(1,128)S(1)}, u32[]{:S(2)}, u32[]{:S(2)}) collective-permute-start(f32[4,4,1,2048]{3,2,1,0:T(1,128)} %get-tuple-element.24), channel_id=1, source_target_pairs={{0,1},{1,2},{2,3},{4,5},{5,6},{6,7},{8,9},{9,10},{10,11},{12,13},{... | collective-permute-start | bytes 393224 | tf_op jit(solution)/shard_map/ppermute | solution.py:24
  427.3 12.3 %collective-permute-start.7 = (f32[4,4,1,2048]{3,2,1,0:T(1,128)}, f32[4,4,1,2048]{3,2,1,0:T(1,128)}, u32[]{:S(2)}, u32[]{:S(2)}) collective-permute-start(f32[4,4,1,2048]{3,2,1,0:T(1,128)} %get-tuple-element.23), channel_id=1, source_target_pairs={{1,0},{2,1},{3,2},{5,4},{6,5},{7,6},{9,8},{10,9},{11,10},{13,12},{... | collective-permute-start | bytes 393224 | tf_op jit(solution)/shard_map/ppermute | solution.py:26
  439.6 12.3 %copy-start.12 = (f32[4]{0:T(128)S(1)}, f32[4]{0:T(128)}, u32[]{:S(2)}) copy-start(f32[4]{0:T(128)} %copy-done.11) | copy-start | bytes 52
  439.6 12.3 %copy-start.14 = (f32[4]{0:T(128)S(1)}, f32[4]{0:T(128)}, u32[]{:S(2)}) copy-start(f32[4]{0:T(128)} %copy-done.13) | copy-start | bytes 52
  458.3 4.9 copy-start.9
  468.3 5.5 copy-start.4
  468.3 5.5 copy-start.6
  491.2 8.7 collective-permute-start.9
  502.9 2.2 copy-start
  507.0 91.0 %collective-permute-start.10 = (f32[4,4,32,2048]{3,2,1,0:T(8,128)S(1)}, f32[4,4,32,2048]{3,2,1,0:T(8,128)S(1)}, u32[]{:S(2)}, u32[]{:S(2)}) collective-permute-start(f32[4,4,32,2048]{3,2,1,0:T(8,128)S(1)} %add_select_fusion.3), channel_id=1, source_target_pairs={{0,8},{4,12},{8,0},{12,4},{16,24},{20,28},{24,16},{28,20},{32,40},... | collective-permute-start | bytes 12582920 | tf_op jit(solution)/shard_map/ppermute | solution.py:36
  601.8 93.9 %collective-permute-start.11 = (f32[4,4,32,2048]{3,2,1,0:T(8,128)S(1)}, f32[4,4,32,2048]{3,2,1,0:T(8,128)S(1)}, u32[]{:S(2)}, u32[]{:S(2)}) collective-permute-start(f32[4,4,32,2048]{3,2,1,0:T(8,128)S(1)} %add_select_fusion.2), channel_id=1, source_target_pairs={{0,16},{4,20},{8,24},{12,28},{16,0},{20,4},{24,8},{28,12},{32,48},... | collective-permute-start | bytes 12582920 | tf_op jit(solution)/shard_map/ppermute | solution.py:36
  698.9 91.8 %collective-permute-start.12 = (f32[4,4,32,2048]{3,2,1,0:T(8,128)S(1)}, f32[4,4,32,2048]{3,2,1,0:T(8,128)S(1)}, u32[]{:S(2)}, u32[]{:S(2)}) collective-permute-start(f32[4,4,32,2048]{3,2,1,0:T(8,128)S(1)} %add_select_fusion.1), channel_id=1, source_target_pairs={{0,32},{4,36},{8,40},{12,44},{16,48},{20,52},{24,56},{28,60},{32,0... | collective-permute-start | bytes 12582920 | tf_op jit(solution)/shard_map/ppermute | solution.py:36
  793.9 92.4 %collective-permute-start.13 = (f32[4,4,32,2048]{3,2,1,0:T(8,128)S(1)}, f32[4,4,32,2048]{3,2,1,0:T(8,128)S(1)}, u32[]{:S(2)}, u32[]{:S(2)}) collective-permute-start(f32[4,4,32,2048]{3,2,1,0:T(8,128)S(1)} %add_select_fusion), channel_id=1, source_target_pairs={{0,64},{4,68},{8,72},{12,76},{16,80},{20,84},{24,88},{28,92},{32,9... | collective-permute-start | bytes 12582920 | tf_op jit(solution)/shard_map/ppermute | solution.py:36
where the time goes:
time: 900 us; the launch traced here: 890 us
  waiting for transfers between devices  679 us (75%)
  other arithmetic  98.3 us (11%)
  local copies, waits for them, and re-layouts  42 us (5%)
  matrix products  35.5 us (4%)
  starting transfers between devices  33.5 us (4%)
    ppermute x10, waiting for transfers between devices, swapped(): return lax.ppermute(value, axis, pairs)  678 us
    dot_general x8, matrix products, mix_rows(): jnp.einsum('ab,sbm->sam', matrix, data, precision=lax.Precision.HIGHEST)  35.5 us
    select_n x4, other arithmetic, body(): data = jnp.where(high, turned, data + partner)  23.9 us
    ppermute x10, starting transfers between devices, swapped(): return lax.ppermute(value, axis, pairs)  23.7 us
  transfers between devices with their start and end apart: 14, of which 10 were waited for; matrix products, arithmetic and copies ran while one was open for 2% of the time, Pallas kernels for 0%

commit v1 on v0

v1 whole, which is shorter than its diff:
```python
import functools
import math

import jax
import jax.numpy as jnp
from jax import lax
from jax.experimental import pallas as pl
from jax.experimental.pallas import tpu as pltpu
from jax.sharding import PartitionSpec as P

NY = 64
COL = 128
ALPHA = 0.1
HALF = 0.5


def turn(value, shift, axis):
    return pltpu.roll(value, (-shift) % value.shape[axis], axis)


def kernel(
    chips, slabs, cells, times,
    state_hbm, adjoint_hbm, kappa_hbm, speed_hbm,
    state_out, adjoint_out,
    rhs, first, result, kappa, speed, couple, solve, power,
    carry_out, carry_in, entry_out, entry_in, edge_out, edge_in,
    load_sem, rhs_send, rhs_recv, kappa_send, kappa_recv,
    carry_send, carry_recv, entry_send, entry_recv,
    edge_send, edge_recv, store_sem, give_send, give_recv,
):
    half_times = times // 2
    lanes = chips // 2
    width = cells // lanes
    columns = width // COL
    total = chips * times
    ratio = ALPHA ** (1.0 / total)

    me = lax.axis_index("tm")
    slab = lax.axis_index("gz")
    chip = me // 2
    core = me % 2
    pair = {"tm": chip * 2 + 1 - core, "gz": slab}
    beside = {"tm": chip * 2 + 1 - core, "gz": (slab + slabs + 2 * core - 1) % slabs}

    def peer(other):
        return {"tm": other * 2 + core, "gz": slab}

    rows = pl.ds(pl.multiple_of(core * 16, 16), 16)
    rows_pair = pl.ds(pl.multiple_of(16 - core * 16, 16), 16)
    own_times = pl.ds(core * half_times, half_times)
    pair_times = pl.ds((1 - core) * half_times, half_times)

    def tile8(start):
        return pl.ds(pl.multiple_of(start, 8), 8)

    loads = [
        pltpu.make_async_copy(kappa_hbm.at[rows], kappa.at[pl.ds(8, 16)], load_sem.at[0]),
        pltpu.make_async_copy(
            kappa_hbm.at[tile8(16 - 8 * core)], kappa.at[tile8(24 - 24 * core)], load_sem.at[1]
        ),
        pltpu.make_async_copy(speed_hbm.at[:, rows], speed, load_sem.at[2]),
        pltpu.make_async_copy(state_hbm.at[:, rows], rhs.at[0, own_times], load_sem.at[3]),
        pltpu.make_async_copy(adjoint_hbm.at[:, rows], rhs.at[1, own_times], load_sem.at[4]),
    ]
    for load in loads:
        load.start()

    barrier = pltpu.get_barrier_semaphore()
    pl.semaphore_signal(barrier, inc=1, device_id=pair)
    pl.semaphore_signal(barrier, inc=1, device_id=beside)

    def greet(step, _):
        pl.semaphore_signal(barrier, inc=1, device_id=peer((chip + step) % chips))
        return 0

    lax.fori_loop(1, chips, greet, 0)
    pl.semaphore_wait(barrier, chips + 1)

    kappa_copy = pltpu.make_async_remote_copy(
        src_ref=kappa_hbm.at[tile8(24 * core)],
        dst_ref=kappa.at[tile8(24 - 24 * core)],
        send_sem=kappa_send,
        recv_sem=kappa_recv,
        device_id=beside,
    )
    kappa_copy.start()
    rhs_copies = []
    for field, source in enumerate((state_hbm, adjoint_hbm)):
        rhs_copies.append(
            pltpu.make_async_remote_copy(
                src_ref=source.at[:, rows_pair],
                dst_ref=rhs.at[field, own_times],
                send_sem=rhs_send.at[field],
                recv_sem=rhs_recv.at[field],
                device_id=pair,
            )
        )
        rhs_copies[field].start()

    lane = lax.broadcasted_iota(jnp.int32, (8, COL), 1)
    row = lax.broadcasted_iota(jnp.int32, (8, COL), 0)
    left = lane < 64
    first_row = row == 0
    last_row = row == 7

    zero = jnp.zeros((8, COL), jnp.float32)
    for field in range(2):
        for step in range(times):
            for z in range(2):
                first[field, step, z * 8 : z * 8 + 8, :COL] = zero
                first[field, step, z * 8 : z * 8 + 8, cells + COL :] = zero

    for load in loads[:3]:
        load.wait()
    kappa_copy.wait_recv()

    def coefficients(k, _):
        lane0 = pl.multiple_of(k * COL, COL)
        here = pl.ds(lane0, COL)
        before = pl.ds(pl.multiple_of(((k + cells // COL - 1) % (cells // COL)) * COL, COL), COL)
        after = pl.ds(pl.multiple_of(((k + 1) % (cells // COL)) * COL, COL), COL)
        x_place = k * 2 + lane // NY
        y_place = lane % NY
        for z in range(2):
            z_place = slab * 32 + core * 16 + z * 8 + row
            own = kappa[8 + z * 8 : 16 + z * 8, here]
            turned = turn(own, 64, 1)
            x_ahead = jnp.where(left, turned, turn(kappa[8 + z * 8 : 16 + z * 8, after], 64, 1))
            x_behind = jnp.where(left, turn(kappa[8 + z * 8 : 16 + z * 8, before], 64, 1), turned)
            z_ahead = jnp.where(
                last_row, turn(kappa[16 + z * 8 : 24 + z * 8, here], 1, 0), turn(own, 1, 0)
            )
            z_behind = jnp.where(
                first_row, turn(kappa[z * 8 : z * 8 + 8, here], -1, 0), turn(own, -1, 0)
            )
            diagonal = jnp.zeros((8, COL), jnp.float32)
            there = pl.ds(z * 8, 8)
            for direction, (ahead, behind, place, count, component) in enumerate(
                (
                    (z_ahead, z_behind, z_place, slabs * 32, 2),
                    (x_ahead, x_behind, x_place, cells // NY, 0),
                    (turn(own, 1, 1), turn(own, -1, 1), y_place, NY, 1),
                )
            ):
                has_ahead = place < count - 1
                has_behind = place > 0
                face_ahead = jnp.where(has_ahead, 0.5 * (own + ahead), own)
                face_behind = jnp.where(has_behind, 0.5 * (own + behind), own)
                diagonal = diagonal + face_ahead + face_behind
                drift = 0.5 * speed[component, there, here]
                couple[0, direction, 0, there, here] = jnp.where(has_ahead, face_ahead - drift, 0.0)
                couple[0, direction, 1, there, here] = jnp.where(has_behind, face_behind + drift, 0.0)
                couple[1, direction, 0, there, here] = jnp.where(has_ahead, face_ahead + drift, 0.0)
                couple[1, direction, 1, there, here] = jnp.where(has_behind, face_behind - drift, 0.0)
            large = 1.0 + diagonal
            over = 1.0 / (large * ratio)
            minus = ((large - ratio) * (large - ratio) + HALF * HALF) * over
            plus = minus + 4.0
            root = 2.0 / (minus + 2.0 + jnp.sqrt(minus * plus))
            lead = large - ratio * root
            gain = root * over / (1.0 - root * root)
            solve[0, there, here] = lead
            solve[1, there, here] = root * (1.0 / ratio)
            solve[2, there, here] = root * ratio
            solve[3, there, here] = gain
            solve[4, there, here] = gain * (HALF / lead)
            solve[5, there, here] = over * ratio
            block = z * lanes + k // columns
            inside = pl.ds(pl.multiple_of((k % columns) * COL, COL), COL)
            for index, base in ((0, root * (1.0 / ratio)), (1, root * ratio)):
                square = base * base
                fourth = square * square
                power[block, index, :, inside] = fourth * fourth
        return 0

    lax.fori_loop(0, cells // COL, coefficients, 0)

    for load in loads[3:]:
        load.wait()
    for copy in rhs_copies:
        copy.wait_recv()

    lane_mine = chip % lanes

    def carry_copy(sweep, other):
        return pltpu.make_async_remote_copy(
            src_ref=carry_out.at[sweep, other],
            dst_ref=carry_in.at[sweep, chip],
            send_sem=carry_send.at[sweep, other],
            recv_sem=carry_recv.at[sweep, chip],
            device_id=peer(other),
        )

    def entry_copy(sweep, other):
        return pltpu.make_async_remote_copy(
            src_ref=entry_out.at[sweep, other],
            dst_ref=entry_in.at[sweep, chip],
            send_sem=entry_send.at[sweep, other],
            recv_sem=entry_recv.at[sweep, chip],
            device_id=peer(other),
        )

    def carry_arrival(sweep, other):
        return pltpu.make_async_remote_copy(
            src_ref=carry_out.at[sweep, other],
            dst_ref=carry_in.at[sweep, other],
            send_sem=carry_send.at[sweep, other],
            recv_sem=carry_recv.at[sweep, other],
            device_id=peer(other),
        )

    def entry_arrival(sweep, other):
        return pltpu.make_async_remote_copy(
            src_ref=entry_out.at[sweep, other],
            dst_ref=entry_in.at[sweep, other],
            send_sem=entry_send.at[sweep, other],
            recv_sem=entry_recv.at[sweep, other],
            device_id=peer(other),
        )

    def send_carry(sweep, block):
        @pl.when(block != chip)
        def _():
            carry_copy(sweep, block).start()

        @pl.when(block == chip)
        def _():
            carry_in[sweep, chip] = carry_out[sweep, block]

    def exchange(sweep):
        def arrive(step, _):
            carry_arrival(sweep, (chip + step) % chips).wait_recv()
            return 0

        lax.fori_loop(1, chips, arrive, 0)
        forward = power[chip, 0]
        backward = power[chip, 1]
        forward_all, backward_all = forward, backward
        for _ in range(chips.bit_length() - 1):
            forward_all = forward_all * forward_all
            backward_all = backward_all * backward_all
        run_forward = carry_in[sweep, 0, 0]
        run_backward = carry_in[sweep, chips - 1, 1]
        for step in range(1, chips):
            run_forward = carry_in[sweep, step, 0] + forward * run_forward
            run_backward = carry_in[sweep, chips - 1 - step, 1] + backward * run_backward
        enter_forward = ALPHA * (run_forward / (1.0 - ALPHA * forward_all))
        enter_backward = (1.0 / ALPHA) * (run_backward / (1.0 - (1.0 / ALPHA) * backward_all))
        entry_out[sweep, 0, 0] = enter_forward
        entry_out[sweep, chips - 1, 1] = enter_backward
        for step in range(1, chips):
            enter_forward = carry_in[sweep, step - 1, 0] + forward * enter_forward
            enter_backward = carry_in[sweep, chips - step, 1] + backward * enter_backward
            entry_out[sweep, step, 0] = enter_forward
            entry_out[sweep, chips - 1 - step, 1] = enter_backward
        entry_in[sweep, chip] = entry_out[sweep, chip]

        def give(step, _):
            entry_copy(sweep, (chip + step) % chips).start()
            return 0

        lax.fori_loop(1, chips, give, 0)

    def await_entry(sweep, block):
        @pl.when(block != chip)
        def _():
            entry_arrival(sweep, block).wait_recv()

    def sums(values, forward, backward):
        ahead = values[0]
        behind = values[-1]
        for step in range(1, times):
            ahead = values[step] + forward * ahead
            behind = values[times - 1 - step] + backward * behind
        return ahead, behind

    def first_sums(step, _):
        block_lane = (lane_mine + step) % lanes
        for column in range(columns):
            here = pl.ds(pl.multiple_of(block_lane * width + column * COL, COL), COL)
            inside = slice(column * COL, column * COL + COL)
            for z in range(2):
                there = slice(z * 8, z * 8 + 8)
                lead = solve[0, there, here]
                forward = solve[1, there, here]
                backward = solve[2, there, here]
                sides = [
                    sums([rhs[field, j, there, here] for j in range(times)], forward, backward)
                    for field in range(2)
                ]
                block = z * lanes + block_lane
                carry_out[0, block, 0, :, inside] = lead * sides[0][0] + HALF * sides[1][0]
                carry_out[0, block, 1, :, inside] = lead * sides[1][1] - HALF * sides[0][1]
        for z in range(2):
            send_carry(0, z * lanes + block_lane)
        return 0

    lax.fori_loop(0, lanes, first_sums, 0)
    exchange(0)

    def solved(sweep, block_lane, column, z, emit):
        here = pl.ds(pl.multiple_of(block_lane * width + column * COL, COL), COL)
        inside = slice(column * COL, column * COL + COL)
        there = slice(z * 8, z * 8 + 8)
        block = z * lanes + block_lane
        lead = solve[0, there, here]
        forward = solve[1, there, here]
        backward = solve[2, there, here]
        gain = solve[3, there, here]
        cross = solve[4, there, here]
        plain = solve[5, there, here]
        back = entry_in[sweep, block, 1, :, inside]
        backs = [None] * times
        for j in reversed(range(times)):
            backs[j] = backward * back
            back = (
                lead * rhs[1, j, there, here] - HALF * rhs[0, j, there, here] + backs[j]
            )
        ahead = entry_in[sweep, block, 0, :, inside]
        for j in range(times):
            adjoint = rhs[1, j, there, here]
            ahead = lead * rhs[0, j, there, here] + HALF * adjoint + forward * ahead
            emit(
                j,
                gain * ahead + cross * backs[j],
                gain * backs[j] - cross * ahead + plain * adjoint,
            )

    def edge_copies(block_lane):
        part = pl.ds(pl.multiple_of(block_lane * width, width), width)
        return (
            pltpu.make_async_remote_copy(
                src_ref=edge_out.at[core, :, part],
                dst_ref=edge_in.at[1 - core, :, part],
                send_sem=edge_send.at[0, block_lane],
                recv_sem=edge_recv.at[0, block_lane],
                device_id=beside,
            ),
            pltpu.make_async_remote_copy(
                src_ref=edge_out.at[1 - core, :, part],
                dst_ref=edge_in.at[core, :, part],
                send_sem=edge_send.at[1, block_lane],
                recv_sem=edge_recv.at[1, block_lane],
                device_id=pair,
            ),
        )

    def first_values(step, _):
        block_lane = (lane_mine + step) % lanes
        for z in range(2):
            await_entry(0, z * lanes + block_lane)
            for column in range(columns):
                shifted = pl.ds(pl.multiple_of(block_lane * width + column * COL + COL, COL), COL)
                here = pl.ds(pl.multiple_of(block_lane * width + column * COL, COL), COL)

                def emit(j, state, adjoint):
                    first[0, j, z * 8 : z * 8 + 8, shifted] = state
                    first[1, j, z * 8 : z * 8 + 8, shifted] = adjoint
                    edge = slice(7 * z, 7 * z + 1)
                    edge_out[z, j : j + 1, here] = state[edge]
                    edge_out[z, times + j : times + j + 1, here] = adjoint[edge]

                solved(0, block_lane, column, z, emit)
        for copy in edge_copies(block_lane):
            copy.start()
        return 0

    lax.fori_loop(0, lanes, first_values, 0)

    def second_sums(step, _):
        block_lane = (lane_mine + step) % lanes
        for copy in edge_copies(block_lane):
            copy.wait_recv()
        for column in range(columns):
            lane0 = block_lane * width + column * COL
            here = pl.ds(pl.multiple_of(lane0, COL), COL)
            shifted = pl.ds(pl.multiple_of(lane0 + COL, COL), COL)
            before = here
            after = pl.ds(pl.multiple_of(lane0 + 2 * COL, COL), COL)
            inside = slice(column * COL, column * COL + COL)
            tiles = (slice(0, 8), slice(8, 16))
            forward = [solve[1, there, here] for there in tiles]
            backward = [solve[2, there, here] for there in tiles]
            sides = []
            for field in range(2):
                weights = [
                    [couple[field, d, s, there, here] for there in tiles]
                    for d in range(3)
                    for s in range(2)
                ]
                ahead_sum = [zero, zero]
                behind_sum = [zero, zero]
                scale = [jnp.ones((8, COL), jnp.float32)] * 2
                for j in range(times):
                    line = field * times + j
                    below = jnp.broadcast_to(edge_in[0, line : line + 1, here], (8, COL))
                    above = jnp.broadcast_to(edge_in[1, line : line + 1, here], (8, COL))
                    own = [first[field, j, there, shifted] for there in tiles]
                    up = [turn(value, 1, 0) for value in own]
                    down = [turn(value, -1, 0) for value in own]
                    z_ahead = [jnp.where(last_row, up[1], up[0]), jnp.where(last_row, above, up[1])]
                    z_behind = [
                        jnp.where(first_row, below, down[0]),
                        jnp.where(first_row, down[0], down[1]),
                    ]
                    for z in range(2):
                        there = tiles[z]
                        turned = turn(own[z], 64, 1)
                        x_ahead = jnp.where(left, turned, turn(first[field, j, there, after], 64, 1))
                        x_behind = jnp.where(left, turn(first[field, j, there, before], 64, 1), turned)
                        value = (
                            rhs[field, j, there, here]
                            + weights[0][z] * z_ahead[z]
                            + weights[1][z] * z_behind[z]
                            + weights[2][z] * x_ahead
                            + weights[3][z] * x_behind
                            + weights[4][z] * turn(own[z], 1, 1)
                            + weights[5][z] * turn(own[z], -1, 1)
                        )
                        rhs[field, j, there, here] = value
                        ahead_sum[z] = value + forward[z] * ahead_sum[z]
                        behind_sum[z] = behind_sum[z] + scale[z] * value
                        if j < times - 1:
                            scale[z] = scale[z] * backward[z]
                sides.append((ahead_sum, behind_sum))
            for z in range(2):
                lead = solve[0, tiles[z], here]
                block = z * lanes + block_lane
                carry_out[1, block, 0, :, inside] = lead * sides[0][0][z] + HALF * sides[1][0][z]
                carry_out[1, block, 1, :, inside] = lead * sides[1][1][z] - HALF * sides[0][1][z]
        for z in range(2):
            send_carry(1, z * lanes + block_lane)
        return 0

    lax.fori_loop(0, lanes, second_sums, 0)
    exchange(1)

    def store_copies(block_lane):
        part = pl.ds(pl.multiple_of(block_lane * width, width), width)
        copies = []
        for field, target in enumerate((state_out, adjoint_out)):
            copies.append(
                pltpu.make_async_copy(
                    result.at[field, own_times, :, part],
                    target.at[:, rows, part],
                    store_sem.at[field, block_lane],
                )
            )
        return copies

    def give_copies(block_lane):
        part = pl.ds(pl.multiple_of(block_lane * width, width), width)
        copies = []
        for field, target in enumerate((state_out, adjoint_out)):
            copies.append(
                pltpu.make_async_remote_copy(
                    src_ref=result.at[field, pair_times, :, part],
                    dst_ref=target.at[:, rows, part],
                    send_sem=give_send.at[field, block_lane],
                    recv_sem=give_recv.at[field, block_lane],
                    device_id=pair,
                )
            )
        return copies

    def second_values(step, _):
        block_lane = (lane_mine + step) % lanes
        for z in range(2):
            await_entry(1, z * lanes + block_lane)
            for column in range(columns):
                here = pl.ds(pl.multiple_of(block_lane * width + column * COL, COL), COL)

                def emit(j, state, adjoint):
                    result[0, j, z * 8 : z * 8 + 8, here] = state
                    result[1, j, z * 8 : z * 8 + 8, here] = adjoint

                solved(1, block_lane, column, z, emit)
        for copy in give_copies(block_lane):
            copy.start()
        for copy in store_copies(block_lane):
            copy.start()
        return 0

    lax.fori_loop(0, lanes, second_values, 0)

    kappa_copy.wait_send()
    for copy in rhs_copies:
        copy.wait_send()

    def sent(step, _):
        other = (chip + step) % chips
        for sweep in range(2):
            carry_copy(sweep, other).wait_send()
            entry_copy(sweep, other).wait_send()
        return 0

    lax.fori_loop(1, chips, sent, 0)

    def stored(block_lane, _):
        for copy in edge_copies(block_lane):
            copy.wait_send()
        for copy in give_copies(block_lane):
            copy.wait_send()
            copy.wait_recv()
        for copy in store_copies(block_lane):
            copy.wait()
        return 0

    lax.fori_loop(0, lanes, stored, 0)


def solution(mesh):
    ranks = mesh.shape["tm"]
    slabs = mesh.shape["gz"]
    chips = ranks // 2

    def body(state_rhs, adjoint_rhs, diffusivity, velocity):
        steps, depth, cells = state_rhs.shape
        times = 2 * steps
        lanes = chips // 2
        width = cells // lanes
        f32 = jnp.float32
        dma = pltpu.SemaphoreType.DMA
        anywhere = pl.BlockSpec(memory_space=pl.ANY)
        exchanged = pltpu.VMEM((2, chips, 2, 8, width), f32)
        call = pl.pallas_call(
            functools.partial(kernel, chips, slabs, cells, times),
            out_shape=[jax.ShapeDtypeStruct(state_rhs.shape, f32)] * 2,
            in_specs=[anywhere] * 4,
            out_specs=[anywhere] * 2,
            scratch_shapes=[
                pltpu.VMEM((2, times, 16, cells), f32),
                pltpu.VMEM((2, times, 16, cells + 2 * COL), f32),
                pltpu.VMEM((2, times, 16, cells), f32),
                pltpu.VMEM((32, cells), f32),
                pltpu.VMEM((3, 16, cells), f32),
                pltpu.VMEM((2, 3, 2, 16, cells), f32),
                pltpu.VMEM((6, 16, cells), f32),
                pltpu.VMEM((chips, 2, 8, width), f32),
                exchanged,
                exchanged,
                exchanged,
                exchanged,
                pltpu.VMEM((2, 2 * times, cells), f32),
                pltpu.VMEM((2, 2 * times, cells), f32),
                dma((5,)),
                dma((2,)),
                dma((2,)),
                dma,
                dma,
                dma((2, chips)),
                dma((2, chips)),
                dma((2, chips)),
                dma((2, chips)),
                dma((2, lanes)),
                dma((2, lanes)),
                dma((2, lanes)),
                dma((2, lanes)),
                dma((2, lanes)),
            ],
            compiler_params=pltpu.CompilerParams(
                collective_id=0, has_side_effects=True, vmem_limit_bytes=40 * 1024 * 1024
            ),
            cost_estimate=pl.CostEstimate(
                flops=60 * state_rhs.size, bytes_accessed=20 * state_rhs.size, transcendentals=0
            ),
        )
        return tuple(call(state_rhs, adjoint_rhs, diffusivity, velocity))

    placed = (P("tm", "gz", None), P("tm", "gz", None), P("gz", None), P(None, "gz", None))
    return jax.shard_map(
        body,
        mesh=mesh,
        in_specs=placed,
        out_specs=(P("tm", "gz", None), P("tm", "gz", None)),
        check_vma=False,
    )
```

time: 900 us -> 51.7 us (0.06); the launches traced: 890 us -> 51.4 us
  waiting for transfers between devices: 679 us -> 0 us
  other arithmetic: 98.3 us -> 0 us
  Pallas kernels: 0 us -> 44.3 us
  local copies, waits for them, and re-layouts: 42 us -> 6.47 us
  matrix products: 35.5 us -> 0 us
  starting transfers between devices: 33.5 us -> 0 us
    ppermute x14 -> x0, waiting for transfers between devices: 679 us -> none  [the longest x10 678 us: swapped(): return lax.ppermute(value, axis, pairs)]
    pallas_call x0 -> x1, Pallas kernels: none -> 44.3 us  [body(): return tuple(call(state_rhs, adjoint_rhs, diffusivity, velocity))]
    select_n x14 -> x0, other arithmetic: 40.1 us -> none  [the longest x4 23.9 us: body(): data = jnp.where(high, turned, data + partner)]
    dot_general x8 -> x0, matrix products: 35.5 us -> none  [mix_rows(): jnp.einsum('ab,sbm->sam', matrix, data, precision=lax.Precision.HIGHEST)]
    ppermute x14 -> x0, starting transfers between devices: 33.5 us -> none  [the longest x10 23.7 us: swapped(): return lax.ppermute(value, axis, pairs)]
    slice x12 -> x0, local copies, waits for them, and re-layouts: 25.2 us -> none  [the longest x2 9.67 us: ahead_flat(): field[..., stride:]]
    sub x9 -> x0, other arithmetic: 19.4 us -> none  [the longest x4 16.3 us: body(): spread = partner - data]
    add x7 -> x0, other arithmetic: 16.2 us -> none  [the longest x1 12.3 us: body(): blocks + coupling(first, first_pad, weights, velocity, NY)]
  transfers between devices with their start and end apart: 14 -> 0, of which waited for: 10 -> 0; matrix products, arithmetic and copies ran while one was open for 2% -> 0% of each run, Pallas kernels for 0% -> 0%
where the time goes in v1:
time: 51.7 us; the launch traced here: 51.4 us
  Pallas kernels  44.3 us (86%)
  local copies, waits for them, and re-layouts  6.47 us (13%)
  between operations  0.65 us (1%)
    pallas_call x1, Pallas kernels, body(): return tuple(call(state_rhs, adjoint_rhs, diffusivity, velocity))  44.3 us
    unnamed x10, local copies, waits for them, and re-layouts  6.47 us

profile of v1, /device:TPU:1, one launch (start us, length us, event | category | flops | bytes accessed | tf_op | source)
XLA Modules:
  0.0 51.4 jit_solution(16058428626654587870)
XLA Ops:
  0.6 0.0 copy-start
  0.6 1.2 %copy-done = f32[4,32,2048]{2,1,0:T(8,128)S(1)} copy-done((f32[4,32,2048]{2,1,0:T(8,128)S(1)}, f32[4,32,2048]{2,1,0:T(8,128)}, u32[]{:S(2)}) %copy-start) | copy-done | bytes 1048600
  1.9 0.0 copy-start.1
  1.9 1.2 %copy-done.1 = f32[4,32,2048]{2,1,0:T(8,128)S(1)} copy-done((f32[4,32,2048]{2,1,0:T(8,128)S(1)}, f32[4,32,2048]{2,1,0:T(8,128)}, u32[]{:S(2)}) %copy-start.1) | copy-done | bytes 1048600
  3.1 0.0 copy-start.2
  3.1 1.1 %copy-done.2 = f32[3,32,2048]{2,1,0:T(8,128)S(1)} copy-done((f32[3,32,2048]{2,1,0:T(8,128)S(1)}, f32[3,32,2048]{2,1,0:T(8,128)}, u32[]{:S(2)}) %copy-start.2) | copy-done | bytes 786456
  4.2 0.0 copy-start.3
  4.2 0.9 %copy-done.3 = f32[32,2048]{1,0:T(8,128)S(1)} copy-done((f32[32,2048]{1,0:T(8,128)S(1)}, f32[32,2048]{1,0:T(8,128)}, u32[]{:S(2)}) %copy-start.3) | copy-done | bytes 262168
  5.2 44.3 %shard_map.59 = (f32[4,32,2048]{2,1,0:T(8,128)S(1)}, f32[4,32,2048]{2,1,0:T(8,128)S(1)}) custom-call(f32[4,32,2048]{2,1,0:T(8,128)S(1)} %copy-done, f32[4,32,2048]{2,1,0:T(8,128)S(1)} %copy-done.1, f32[32,2048]{1,0:T(8,128)S(1)} %copy-done.3, f32[3,32,2048]{2,1,0:T(8,128)S(1)} %copy-done.2), custom_call_target="tpu_custom_call" | custom-call | flops 15728640 | bytes 5242880 | tf_op jit(solution)/shard_map/pallas_call | solution.py:568
  49.5 1.0 %copy.8 = f32[4,32,2048]{2,1,0:T(8,128)} copy(f32[4,32,2048]{2,1,0:T(8,128)S(1)} %get-tuple-element.4) | data formatting | bytes 2097152
  50.5 1.0 %copy.9 = f32[4,32,2048]{2,1,0:T(8,128)} copy(f32[4,32,2048]{2,1,0:T(8,128)S(1)} %get-tuple-element.5) | data formatting | bytes 2097152
Async XLA Ops:
  0.6 1.2 %copy-start = (f32[4,32,2048]{2,1,0:T(8,128)S(1)}, f32[4,32,2048]{2,1,0:T(8,128)}, u32[]{:S(2)}) copy-start(f32[4,32,2048]{2,1,0:T(8,128)} %state_hbm.1) | copy-start | bytes 3145732
  1.9 1.2 %copy-start.1 = (f32[4,32,2048]{2,1,0:T(8,128)S(1)}, f32[4,32,2048]{2,1,0:T(8,128)}, u32[]{:S(2)}) copy-start(f32[4,32,2048]{2,1,0:T(8,128)} %adjoint_hbm.1) | copy-start | bytes 3145732
  3.1 1.1 %copy-start.2 = (f32[3,32,2048]{2,1,0:T(8,128)S(1)}, f32[3,32,2048]{2,1,0:T(8,128)}, u32[]{:S(2)}) copy-start(f32[3,32,2048]{2,1,0:T(8,128)} %speed_hbm.1) | copy-start | bytes 2359300
  4.2 0.9 %copy-start.3 = (f32[32,2048]{1,0:T(8,128)S(1)}, f32[32,2048]{1,0:T(8,128)}, u32[]{:S(2)}) copy-start(f32[32,2048]{1,0:T(8,128)} %kappa_hbm.1) | copy-start | bytes 786436

commit v2 on v0

v2 whole, which is shorter than its diff:
```python
import functools
import math

import jax
import jax.numpy as jnp
from jax import lax
from jax.experimental import pallas as pl
from jax.experimental.pallas import tpu as pltpu
from jax.sharding import PartitionSpec as P

NY = 64
COL = 128
ALPHA = 0.1
HALF = 0.5


def turn(value, shift, axis):
    return pltpu.roll(value, (-shift) % value.shape[axis], axis)


def kernel(
    chips, slabs, cells, times,
    state_hbm, adjoint_hbm, kappa_hbm, speed_hbm,
    both_out, gain_out,
    rhs, first, twist, result, kappa, edge_row, rim, speed, couple, solve, power, growth,
    carry_out, carry_in, entry_out, entry_in, edge_out, edge_in,
    load_sem, rhs_send, rhs_recv, kappa_send, kappa_recv, gain_sem,
    carry_send, carry_recv, entry_send, entry_recv,
    edge_send, edge_recv, store_sem, give_send, give_recv,
):
    half_times = times // 2
    lanes = chips // 2
    columns = cells // COL
    groups = columns // lanes
    width = lanes * COL
    total = chips * times
    ratio = ALPHA ** (1.0 / total)

    me = lax.axis_index("tm")
    slab = lax.axis_index("gz")
    chip = me // 2
    core = me % 2
    pair = {"tm": chip * 2 + 1 - core, "gz": slab}
    beside = {"tm": chip * 2 + 1 - core, "gz": (slab + slabs + 2 * core - 1) % slabs}

    behind_same = {"tm": me, "gz": (slab + slabs - 1) % slabs}

    def peer(other):
        return {"tm": other * 2 + core, "gz": slab}

    rows = pl.ds(pl.multiple_of(core * 16, 16), 16)
    rows_pair = pl.ds(pl.multiple_of(16 - core * 16, 16), 16)
    own_times = pl.ds(core * half_times, half_times)
    pair_times = pl.ds((1 - core) * half_times, half_times)

    def tile8(start):
        return pl.ds(pl.multiple_of(start, 8), 8)

    loads = [
        pltpu.make_async_copy(kappa_hbm.at[rows], kappa.at[pl.ds(8, 16)], load_sem.at[0]),
        pltpu.make_async_copy(
            kappa_hbm.at[tile8(16 - 8 * core)], kappa.at[tile8(24 - 24 * core)], load_sem.at[0]
        ),
        pltpu.make_async_copy(kappa_hbm.at[pl.ds(0, 8)], edge_row, load_sem.at[0]),
        pltpu.make_async_copy(speed_hbm.at[:, rows], speed, load_sem.at[1]),
        pltpu.make_async_copy(state_hbm.at[:, rows], rhs.at[0, own_times], load_sem.at[2]),
        pltpu.make_async_copy(adjoint_hbm.at[:, rows], rhs.at[1, own_times], load_sem.at[2]),
    ]
    for load in loads:
        load.start()

    barrier = pltpu.get_barrier_semaphore()
    pl.semaphore_signal(barrier, inc=1, device_id=pair)
    pl.semaphore_signal(barrier, inc=1, device_id=beside)

    @pl.when(core == 1)
    def _():
        pl.semaphore_signal(barrier, inc=1, device_id={"tm": me, "gz": (slab + 1) % slabs})


    def greet(step, _):
        pl.semaphore_signal(barrier, inc=1, device_id=peer((chip + step) % chips))
        return 0

    lax.fori_loop(1, chips, greet, 0)
    def kappa_copy(side):
        return pltpu.make_async_remote_copy(
            src_ref=rim.at[side],
            dst_ref=rim.at[2],
            send_sem=kappa_send,
            recv_sem=kappa_recv,
            device_id=beside if side else behind_same,
        )

    def rhs_copies(group):
        part = slice(group * width, group * width + width)
        return [
            pltpu.make_async_remote_copy(
                src_ref=source.at[:, rows_pair, part],
                dst_ref=rhs.at[field, own_times, :, part],
                send_sem=rhs_send,
                recv_sem=rhs_recv.at[group],
                device_id=pair,
            )
            for field, source in enumerate((state_hbm, adjoint_hbm))
        ]

    def lane_of(half, odd):
        if lanes != 8:
            return (chip + 2 * half + odd) % lanes
        outer = half % 3 == 0
        if isinstance(half, int):
            move_x = 2 - 2 * (half // 3) if outer else 1 + 2 * odd
            move_y = odd if outer else half - 1
        else:
            move_x = jnp.where(outer, 2 - 2 * (half // 3), 1 + 2 * odd)
            move_y = jnp.where(outer, odd, half - 1)
        return ((chip // 4 + move_y) % 2) * 4 + (chip % 4 + move_x) % 4

    pairs = lanes // 2
    classes = (pairs + 1) // 2

    lane = lax.broadcasted_iota(jnp.int32, (8, COL), 1)
    row = lax.broadcasted_iota(jnp.int32, (8, COL), 0)
    left = lane < 64
    first_row = row == 0
    last_row = row == 7

    zero = jnp.zeros((8, COL), jnp.float32)
    for field in range(2):
        for step in range(times):
            for z in range(2):
                twist[field, step, z * 8 : z * 8 + 8, :COL] = zero
                twist[field, step, z * 8 : z * 8 + 8, cells + COL :] = zero

    pltpu.make_async_copy(kappa.at[pl.ds(0, 32)], kappa.at[pl.ds(0, 32)], load_sem.at[0]).wait()
    piece_width = cells // 8

    @pl.when(core == 1)
    def _():
        for side, source, line in ((0, edge_row, 0), (1, kappa, 23)):
            for piece in range(8):
                part = slice(piece * piece_width, piece * piece_width + piece_width)
                rim[side, piece : piece + 1, :] = source[line : line + 1, part]

    loads[3].wait()

    def coefficients(k, z):
        there = pl.ds(pl.multiple_of(z * 8, 8), 8)
        centre = pl.ds(pl.multiple_of(8 + z * 8, 8), 8)
        below = pl.ds(pl.multiple_of(z * 8, 8), 8)
        above = pl.ds(pl.multiple_of(16 + z * 8, 8), 8)
        lane0 = pl.multiple_of(k * COL, COL)
        here = pl.ds(lane0, COL)
        before = pl.ds(pl.multiple_of(((k + cells // COL - 1) % (cells // COL)) * COL, COL), COL)
        after = pl.ds(pl.multiple_of(((k + 1) % (cells // COL)) * COL, COL), COL)
        x_place = k * 2 + lane // NY
        y_place = lane % NY
        z_place = slab * 32 + core * 16 + z * 8 + row
        own = kappa[centre, here]
        turned = turn(own, 64, 1)
        x_ahead = jnp.where(left, turned, turn(kappa[centre, after], 64, 1))
        x_behind = jnp.where(left, turn(kappa[centre, before], 64, 1), turned)
        z_ahead = jnp.where(
            last_row, turn(kappa[above, here], 1, 0), turn(own, 1, 0)
        )
        z_behind = jnp.where(
            first_row, turn(kappa[below, here], -1, 0), turn(own, -1, 0)
        )
        diagonal = jnp.zeros((8, COL), jnp.float32)
        for direction, (ahead, behind, place, count, component) in enumerate(
            (
                (z_ahead, z_behind, z_place, slabs * 32, 2),
                (x_ahead, x_behind, x_place, cells // NY, 0),
                (turn(own, 1, 1), turn(own, -1, 1), y_place, NY, 1),
            )
        ):
            has_ahead = place < count - 1
            has_behind = place > 0
            face_ahead = jnp.where(has_ahead, 0.5 * (own + ahead), own)
            face_behind = jnp.where(has_behind, 0.5 * (own + behind), own)
            diagonal = diagonal + face_ahead + face_behind
            drift = 0.5 * speed[component, there, here]
            couple[0, direction, 0, there, here] = jnp.where(has_ahead, face_ahead - drift, 0.0)
            couple[0, direction, 1, there, here] = jnp.where(has_behind, face_behind + drift, 0.0)
            couple[1, direction, 0, there, here] = jnp.where(has_ahead, face_ahead + drift, 0.0)
            couple[1, direction, 1, there, here] = jnp.where(has_behind, face_behind - drift, 0.0)
        large = 1.0 + diagonal
        over = 1.0 / (large * ratio)
        minus = ((large - ratio) * (large - ratio) + HALF * HALF) * over
        plus = minus + 4.0
        root = 2.0 / (minus + 2.0 + jnp.sqrt(minus * plus))
        lead = large - ratio * root
        gain = root * over / (1.0 - root * root)
        solve[0, there, here] = lead
        solve[1, there, here] = root * (1.0 / ratio)
        solve[2, there, here] = root * ratio
        solve[3, there, here] = gain
        solve[4, there, here] = HALF / lead
        solve[5, there, here] = ratio * (1.0 - root * root) / root
        for index, base in ((0, root * (1.0 / ratio)), (1, root * ratio)):
            square = base * base
            fourth = square * square
            power[k // lanes, z * lanes + k % lanes, index] = fourth * fourth

    def inner_coefficients(step, _):
        for k in range(4):
            coefficients(step * 4 + k, 1 - core)
        return 0

    def outer_coefficients(step, _):
        for k in range(4):
            coefficients(step * 4 + k, core)
        return 0

    lax.fori_loop(0, cells // COL // 4, inner_coefficients, 0)
    pl.semaphore_wait(barrier, chips + 1 + core)

    @pl.when(core == 1)
    def _():
        for side in range(2):
            kappa_copy(side).start()

    for group in range(groups):
        for copy in rhs_copies(group):
            copy.start()

    pltpu.make_async_copy(rhs.at[:, own_times], rhs.at[:, own_times], load_sem.at[2]).wait()
    kappa_copy(1).wait_recv()
    for side in range(2):

        @pl.when(core == side)
        def _():
            for piece in range(8):
                part = slice(piece * piece_width, piece * piece_width + piece_width)
                kappa[7 + 17 * side : 8 + 17 * side, part] = rim[2, piece : piece + 1, :]

    lax.fori_loop(0, cells // COL // 4, outer_coefficients, 0)

    def carry_copy(lot, other):
        return pltpu.make_async_remote_copy(
            src_ref=carry_out.at[lot, other],
            dst_ref=carry_in.at[lot, chip],
            send_sem=carry_send,
            recv_sem=carry_recv.at[lot],
            device_id=peer(other),
        )

    def entry_copy(lot, other, kind):
        return pltpu.make_async_remote_copy(
            src_ref=entry_out.at[lot, other],
            dst_ref=entry_in.at[lot, chip],
            send_sem=entry_send,
            recv_sem=entry_recv.at[lot, kind],
            device_id=peer(other),
        )

    def await_entry(lot, kind):
        def take(count):
            blocks = entry_in.at[lot, pl.ds(0, count)]
            pltpu.make_async_copy(blocks, blocks, entry_recv.at[lot, kind]).wait()

        count = 2 * lanes // classes
        if classes == 1:
            take(count - 1)
        else:

            @pl.when(kind == classes - 1)
            def _():
                take(count - 1)

            @pl.when(kind < classes - 1)
            def _():
                take(count)

    def send_carry(lot, block, odd):
        if odd:
            carry_copy(lot, block).start()
        else:

            @pl.when(block != chip)
            def _():
                carry_copy(lot, block).start()

            @pl.when(block == chip)
            def _():
                carry_in[lot, chip] = carry_out[lot, block]

    def powers(group):
        for direction in range(2):
            factor = power[group, chip, direction]
            run = factor
            for step in range(1, chips + 1):
                growth[group, step, direction] = run
                run = run * factor

    def exchange(sweep, group):
        lot = sweep * groups + group

        arrived = carry_in.at[lot, pl.ds(0, chips - 1)]
        pltpu.make_async_copy(arrived, arrived, carry_recv.at[lot]).wait()
        for direction, wrap in ((0, ALPHA), (1, 1.0 / ALPHA)):
            factor = growth[group, 1, direction]
            order = range(chips) if direction == 0 else range(chips - 1, -1, -1)
            run = None
            before = []
            for place in order:
                before.append(run)
                carry = carry_in[lot, place, direction]
                run = carry if run is None else carry + factor * run
            start = wrap * (run / (1.0 - wrap * growth[group, chips, direction]))
            for step, place in enumerate(order):
                value = start
                if step:
                    value = before[step] + start * growth[group, step, direction]
                entry_out[lot, place, direction] = value
        entry_in[lot, chip] = entry_out[lot, chip]

        for half in range(pairs):
            for odd in range(2):
                for z in range(2):
                    other = z * lanes + lane_of(half, odd)
                    if half == pairs - 1 or lanes != 8:

                        @pl.when(other != chip)
                        def _():
                            entry_copy(lot, other, half // 2).start()

                    else:
                        entry_copy(lot, other, half // 2).start()

    def sums(values, forward, backward):
        ahead = values[0]
        behind = values[-1]
        for step in range(1, times):
            ahead = values[step] + forward * ahead
            behind = values[times - 1 - step] + backward * behind
        return ahead, behind

    gain_store = pltpu.make_async_copy(solve.at[3], gain_out.at[rows], load_sem.at[3])
    gain_give = pltpu.make_async_remote_copy(
        src_ref=solve.at[3],
        dst_ref=gain_out.at[rows],
        send_sem=gain_sem.at[0],
        recv_sem=gain_sem.at[1],
        device_id=pair,
    )

    def first_sums(group):
        def pair_sums(half, _):
            for odd in range(2):
                lane = lane_of(half, odd)
                here = pl.ds(pl.multiple_of(group * width + lane * COL, COL), COL)
                for z in range(2):
                    there = slice(z * 8, z * 8 + 8)
                    lead = solve[0, there, here]
                    forward = solve[1, there, here]
                    backward = solve[2, there, here]
                    sides = [
                        sums([rhs[field, j, there, here] for j in range(times)], forward, backward)
                        for field in range(2)
                    ]
                    block = z * lanes + lane
                    carry_out[group, block, 0] = lead * sides[0][0] + HALF * sides[1][0]
                    carry_out[group, block, 1] = lead * sides[1][1] - HALF * sides[0][1]
            for odd in range(2):
                for z in range(2):
                    send_carry(group, z * lanes + lane_of(half, odd), odd)
            return 0

        lax.fori_loop(0, pairs, pair_sums, 0)

    for group in range(groups):
        arrived = rhs.at[:, own_times, :, slice(0, width)]
        pltpu.make_async_copy(arrived, arrived, rhs_recv.at[group]).wait()
        first_sums(group)
    gain_store.start()
    gain_give.start()
    for group in range(groups):
        powers(group)
    for group in range(groups):
        exchange(0, group)

    def solved(sweep, group, lane, z, emit):
        here = pl.ds(pl.multiple_of(group * width + lane * COL, COL), COL)
        there = slice(z * 8, z * 8 + 8)
        lot = sweep * groups + group
        block = z * lanes + lane
        lead = solve[0, there, here]
        forward = solve[1, there, here]
        backward = solve[2, there, here]
        gain = solve[3, there, here]
        cross = solve[4, there, here]
        plain = solve[5, there, here]
        back = entry_in[lot, block, 1]
        backs = [None] * times
        for j in reversed(range(times)):
            backs[j] = backward * back
            back = (
                lead * rhs[1, j, there, here] - HALF * rhs[0, j, there, here] + backs[j]
            )
        ahead = entry_in[lot, block, 0]
        for j in range(times):
            adjoint = rhs[1, j, there, here]
            ahead = lead * rhs[0, j, there, here] + HALF * adjoint + forward * ahead
            state = ahead + cross * backs[j]
            adjoint = backs[j] - cross * ahead + plain * adjoint
            if sweep == 0:
                state, adjoint = gain * state, gain * adjoint
            emit(j, state, adjoint)

    def edge_copies(column, mark):
        part = pl.ds(pl.multiple_of(column * COL, COL), COL)
        return (
            pltpu.make_async_remote_copy(
                src_ref=edge_out.at[core, :, part],
                dst_ref=edge_in.at[1 - core, :, part],
                send_sem=edge_send,
                recv_sem=edge_recv.at[mark],
                device_id=beside,
            ),
            pltpu.make_async_remote_copy(
                src_ref=edge_out.at[1 - core, :, part],
                dst_ref=edge_in.at[core, :, part],
                send_sem=edge_send,
                recv_sem=edge_recv.at[mark],
                device_id=pair,
            ),
        )

    def first_values(group):
        def pair_values(step, _):
            half = pairs - 1 - step

            @pl.when(step % 2 == 0)
            def _():
                await_entry(group, half // 2)

            for odd in (1, 0):
                lane = lane_of(half, odd)
                column = group * lanes + lane
                here = pl.ds(pl.multiple_of(column * COL, COL), COL)
                shifted = pl.ds(pl.multiple_of(column * COL + COL, COL), COL)
                for z in range(2):

                    def emit(j, state, adjoint):
                        first[0, j, z * 8 : z * 8 + 8, here] = state
                        first[1, j, z * 8 : z * 8 + 8, here] = adjoint
                        twist[0, j, z * 8 : z * 8 + 8, shifted] = turn(state, 64, 1)
                        twist[1, j, z * 8 : z * 8 + 8, shifted] = turn(adjoint, 64, 1)
                        edge = slice(7 * z, 7 * z + 1)
                        edge_out[z, j : j + 1, here] = state[edge]
                        edge_out[z, times + j : times + j + 1, here] = adjoint[edge]

                    solved(0, group, lane, z, emit)
            for odd in (1, 0):
                for copy in edge_copies(group * lanes + lane_of(half, odd), group * classes + half // 2):
                    copy.start()
            return 0

        lax.fori_loop(0, pairs, pair_values, 0)

    for group in range(groups):
        first_values(group)

    def second_sums(group):
        def pair_sums(step, _):
            half = pairs - 1 - step

            @pl.when(step % 2 == 0)
            def _():
                arrived = edge_in.at[:, :, pl.ds(0, 2 * pairs // classes * COL)]
                sem = edge_recv.at[group * classes + half // 2]
                pltpu.make_async_copy(arrived, arrived, sem).wait()

            for odd in (1, 0):
                lane = lane_of(half, odd)
                column = group * lanes + lane
                lane0 = column * COL
                here = pl.ds(pl.multiple_of(lane0, COL), COL)
                shifted = pl.ds(pl.multiple_of(lane0 + COL, COL), COL)
                before = here
                after = pl.ds(pl.multiple_of(lane0 + 2 * COL, COL), COL)
                tiles = (slice(0, 8), slice(8, 16))
                forward = [solve[1, there, here] for there in tiles]
                backward = [solve[2, there, here] for there in tiles]
                sides = []
                for field in range(2):
                    weights = [
                        [couple[field, d, s, there, here] for there in tiles]
                        for d in range(3)
                        for s in range(2)
                    ]
                    ahead_sum = [zero, zero]
                    behind_sum = [zero, zero]
                    scale = [jnp.ones((8, COL), jnp.float32)] * 2
                    for j in range(times):
                        line = field * times + j
                        below = jnp.broadcast_to(edge_in[0, line : line + 1, here], (8, COL))
                        above = jnp.broadcast_to(edge_in[1, line : line + 1, here], (8, COL))
                        own = [first[field, j, there, here] for there in tiles]
                        up = [turn(value, 1, 0) for value in own]
                        down = [turn(value, -1, 0) for value in own]
                        z_ahead = [jnp.where(last_row, up[1], up[0]), jnp.where(last_row, above, up[1])]
                        z_behind = [
                            jnp.where(first_row, below, down[0]),
                            jnp.where(first_row, down[0], down[1]),
                        ]
                        for z in range(2):
                            there = tiles[z]
                            turned = twist[field, j, there, shifted]
                            x_ahead = jnp.where(left, turned, twist[field, j, there, after])
                            x_behind = jnp.where(left, twist[field, j, there, before], turned)
                            value = (
                                rhs[field, j, there, here]
                                + weights[0][z] * z_ahead[z]
                                + weights[1][z] * z_behind[z]
                                + weights[2][z] * x_ahead
                                + weights[3][z] * x_behind
                                + weights[4][z] * turn(own[z], 1, 1)
                                + weights[5][z] * turn(own[z], -1, 1)
                            )
                            rhs[field, j, there, here] = value
                            ahead_sum[z] = value + forward[z] * ahead_sum[z]
                            behind_sum[z] = behind_sum[z] + scale[z] * value
                            if j < times - 1:
                                scale[z] = scale[z] * backward[z]
                    sides.append((ahead_sum, behind_sum))
                for z in range(2):
                    lead = solve[0, tiles[z], here]
                    block = z * lanes + lane
                    lot = groups + group
                    carry_out[lot, block, 0] = lead * sides[0][0][z] + HALF * sides[1][0][z]
                    carry_out[lot, block, 1] = lead * sides[1][1][z] - HALF * sides[0][1][z]
            for odd in (1, 0):
                for z in range(2):
                    send_carry(groups + group, z * lanes + lane_of(half, odd), odd)
            return 0

        lax.fori_loop(0, pairs, pair_sums, 0)

    for group in range(groups):
        second_sums(group)
    for group in range(groups):
        exchange(1, group)

    def store_copy(column):
        part = pl.ds(pl.multiple_of(column * COL, COL), COL)
        return pltpu.make_async_copy(
            result.at[:, own_times, :, part], both_out.at[:, :, rows, part], store_sem
        )

    def give_copy(column):
        part = pl.ds(pl.multiple_of(column * COL, COL), COL)
        return pltpu.make_async_remote_copy(
            src_ref=result.at[:, pair_times, :, part],
            dst_ref=both_out.at[:, :, rows, part],
            send_sem=give_send,
            recv_sem=give_recv,
            device_id=pair,
        )

    def second_values(group):
        def pair_values(step, _):
            half = pairs - 1 - step

            @pl.when(step % 2 == 0)
            def _():
                await_entry(groups + group, half // 2)

            for odd in (1, 0):
                lane = lane_of(half, odd)
                here = pl.ds(pl.multiple_of((group * lanes + lane) * COL, COL), COL)
                for z in range(2):

                    def emit(j, state, adjoint):
                        result[0, j, z * 8 : z * 8 + 8, here] = state
                        result[1, j, z * 8 : z * 8 + 8, here] = adjoint

                    solved(1, group, lane, z, emit)
            for odd in (1, 0):
                give_copy(group * lanes + lane_of(half, odd)).start()
                store_copy(group * lanes + lane_of(half, odd)).start()
            return 0

        lax.fori_loop(0, pairs, pair_values, 0)

    for group in range(groups):
        second_values(group)

    def drain(ref, semaphore):
        pltpu.make_async_copy(ref, ref, semaphore).wait()

    gain_store.wait()
    gain_give.wait()

    @pl.when(core == 1)
    def _():
        drain(rim.at[pl.ds(0, 2)], kappa_send)

    drain(rhs.at[:, own_times], rhs_send)
    drain(carry_out.at[:, pl.ds(0, chips - 1)], carry_send)
    drain(entry_out.at[:, pl.ds(0, chips - 1)], entry_send)
    drain(edge_out, edge_send)
    drain(result.at[:, own_times], give_send)
    drain(result.at[:, own_times], store_sem)
    drain(result.at[:, own_times], give_recv)


def solution(mesh):
    ranks = mesh.shape["tm"]
    slabs = mesh.shape["gz"]
    chips = ranks // 2

    def body(state_rhs, adjoint_rhs, diffusivity, velocity):
        steps, depth, cells = state_rhs.shape
        times = 2 * steps
        columns = cells // COL
        groups = 2 * columns // chips
        f32 = jnp.float32
        dma = pltpu.SemaphoreType.DMA
        anywhere = pl.BlockSpec(memory_space=pl.ANY)
        exchanged = pltpu.VMEM((2 * groups, chips, 2, 8, COL), f32)
        call = pl.pallas_call(
            functools.partial(kernel, chips, slabs, cells, times),
            out_shape=[
                pltpu.VMEM((2, steps, depth, cells), f32),
                pltpu.VMEM((depth, cells), f32),
            ],
            in_specs=[anywhere] * 4,
            out_specs=[anywhere] * 2,
            scratch_shapes=[
                pltpu.VMEM((2, times, 16, cells), f32),
                pltpu.VMEM((2, times, 16, cells), f32),
                pltpu.VMEM((2, times, 16, cells + 2 * COL), f32),
                pltpu.VMEM((2, times, 16, cells), f32),
                pltpu.VMEM((32, cells), f32),
                pltpu.VMEM((8, cells), f32),
                pltpu.VMEM((3, 8, cells // 8), f32),
                pltpu.VMEM((3, 16, cells), f32),
                pltpu.VMEM((2, 3, 2, 16, cells), f32),
                pltpu.VMEM((6, 16, cells), f32),
                pltpu.VMEM((groups, chips, 2, 8, COL), f32),
                pltpu.VMEM((groups, chips + 1, 2, 8, COL), f32),
                exchanged,
                exchanged,
                exchanged,
                exchanged,
                pltpu.VMEM((2, 2 * times, cells), f32),
                pltpu.VMEM((2, 2 * times, cells), f32),
                dma((4,)),
                dma,
                dma((groups,)),
                dma,
                dma,
                dma((2,)),
                dma,
                dma((2 * groups,)),
                dma,
                dma((2 * groups, 2)),
                dma,
                dma((2 * groups,)),
                dma,
                dma,
                dma,
            ],
            compiler_params=pltpu.CompilerParams(
                collective_id=0, has_side_effects=True, vmem_limit_bytes=48 * 1024 * 1024
            ),
            cost_estimate=pl.CostEstimate(
                flops=60 * state_rhs.size, bytes_accessed=20 * state_rhs.size, transcendentals=0
            ),
        )
        held = [
            pltpu.with_memory_space_constraint(array, pltpu.HBM)
            for array in (state_rhs, adjoint_rhs, diffusivity, velocity)
        ]
        both, gain = call(*held)
        return both[0] * gain, both[1] * gain

    placed = (P("tm", "gz", None), P("tm", "gz", None), P("gz", None), P(None, "gz", None))
    return jax.shard_map(
        body,
        mesh=mesh,
        in_specs=placed,
        out_specs=(P("tm", "gz", None), P("tm", "gz", None)),
        check_vma=False,
    )
```

time: 900 us -> 41.7 us (0.05); the launches traced: 890 us -> 41.6 us
  waiting for transfers between devices: 679 us -> 0 us
  other arithmetic: 98.3 us -> 1.56 us
  local copies, waits for them, and re-layouts: 42 us -> 0 us
  Pallas kernels: 0 us -> 39.4 us
  matrix products: 35.5 us -> 0 us
  starting transfers between devices: 33.5 us -> 0 us
    ppermute x14 -> x0, waiting for transfers between devices: 679 us -> none  [the longest x10 678 us: swapped(): return lax.ppermute(value, axis, pairs)]
    select_n x14 -> x0, other arithmetic: 40.1 us -> none  [the longest x4 23.9 us: body(): data = jnp.where(high, turned, data + partner)]
    pallas_call x0 -> x1, Pallas kernels: none -> 39.4 us  [body(): both, gain = call(*held)]
    dot_general x8 -> x0, matrix products: 35.5 us -> none  [mix_rows(): jnp.einsum('ab,sbm->sam', matrix, data, precision=lax.Precision.HIGHEST)]
    ppermute x14 -> x0, starting transfers between devices: 33.5 us -> none  [the longest x10 23.7 us: swapped(): return lax.ppermute(value, axis, pairs)]
    slice x12 -> x0, local copies, waits for them, and re-layouts: 25.2 us -> none  [the longest x2 9.67 us: ahead_flat(): field[..., stride:]]
    sub x9 -> x0, other arithmetic: 19.4 us -> none  [the longest x4 16.3 us: body(): spread = partner - data]
    add x7 -> x0, other arithmetic: 16.2 us -> none  [the longest x1 12.3 us: body(): blocks + coupling(first, first_pad, weights, velocity, NY)]
  transfers between devices with their start and end apart: 14 -> 0, of which waited for: 10 -> 0; matrix products, arithmetic and copies ran while one was open for 2% -> 0% of each run, Pallas kernels for 0% -> 0%
where the time goes in v2:
time: 41.7 us; the launch traced here: 41.6 us
  Pallas kernels  39.4 us (94%)
  other arithmetic  1.56 us (4%)
  between operations  0.64 us (2%)
    pallas_call x1, Pallas kernels, body(): both, gain = call(*held)  39.4 us
    mul x1, other arithmetic, body(): return (both[0] * gain, both[1] * gain)  1.56 us

profile of v2, /device:TPU:1, one launch (start us, length us, event | category | flops | bytes accessed | tf_op | source)
XLA Modules:
  0.0 41.6 jit_solution(6203003090349253085)
XLA Ops:
  0.6 39.4 %shard_map.59 = (f32[2,4,32,2048]{3,2,1,0:T(8,128)S(1)}, f32[32,2048]{1,0:T(8,128)S(1)}) custom-call(f32[4,32,2048]{2,1,0:T(8,128)} %state_hbm.1, f32[4,32,2048]{2,1,0:T(8,128)} %adjoint_hbm.1, f32[32,2048]{1,0:T(8,128)} %kappa_hbm.1, f32[3,32,2048]{2,1,0:T(8,128)} %speed_hbm.1), custom_call_target="tpu_custom_call" | custom-call | flops 15728640 | bytes 5242880 | tf_op jit(solution)/shard_map/pallas_call | solution.py:678
  40.0 1.6 %bitcast_multiply_fusion = (f32[4,32,2048]{2,1,0:T(8,128)}, f32[4,32,2048]{2,1,0:T(8,128)}) fusion(f32[2,4,32,2048]{3,2,1,0:T(8,128)S(1)} %get-tuple-element.4, f32[32,2048]{1,0:T(8,128)S(1)} %get-tuple-element.5), kind=kLoop, calls=%fused_computation | loop fusion | flops 524288 | bytes 4456448 | tf_op jit(solution)/shard_map/mul | solution.py:679

commit v3 on v2

--- a/solution.py
+++ b/solution.py
@@ -22,9 +22,9 @@
     chips, slabs, cells, times,
     state_hbm, adjoint_hbm, kappa_hbm, speed_hbm,
     both_out, gain_out,
-    rhs, first, twist, result, kappa, edge_row, rim, speed, couple, solve, power, growth,
+    rhs, first, twist, result, kappa, edge_row, rim, speed, couple, solve, power, base, growth,
     carry_out, carry_in, entry_out, entry_in, edge_out, edge_in,
-    load_sem, rhs_send, rhs_recv, kappa_send, kappa_recv, gain_sem,
+    load_sem, rhs_send, rhs_recv, kappa_send, kappa_recv, gain_sem, base_sem,
     carry_send, carry_recv, entry_send, entry_recv,
     edge_send, edge_recv, store_sem, give_send, give_recv,
 ):
@@ -46,12 +46,27 @@
     behind_same = {"tm": me, "gz": (slab + slabs - 1) % slabs}
 
     def peer(other):
-        return {"tm": other * 2 + core, "gz": slab}
+        return {"tm": other * 2 + 1 - core, "gz": slab}
 
     rows = pl.ds(pl.multiple_of(core * 16, 16), 16)
     rows_pair = pl.ds(pl.multiple_of(16 - core * 16, 16), 16)
     own_times = pl.ds(core * half_times, half_times)
     pair_times = pl.ds((1 - core) * half_times, half_times)
+
+    def lane_of(half, odd):
+        if lanes != 8:
+            return (chip + 2 * half + odd) % lanes
+        outer = half % 3 == 0
+        if isinstance(half, int):
+            move_x = 2 - 2 * (half // 3) if outer else 1 + 2 * odd
+            move_y = odd if outer else half - 1
+        else:
+            move_x = jnp.where(outer, 2 - 2 * (half // 3), 1 + 2 * odd)
+            move_y = jnp.where(outer, odd, half - 1)
+        return ((chip // 4 + move_y) % 2) * 4 + (chip % 4 + move_x) % 4
+
+    pairs = lanes // 2
+    classes = (pairs + 1) // 2
 
     def tile8(start):
         return pl.ds(pl.multiple_of(start, 8), 8)
@@ -70,19 +85,17 @@
         load.start()
 
     barrier = pltpu.get_barrier_semaphore()
-    pl.semaphore_signal(barrier, inc=1, device_id=pair)
+    for half in range(lanes // 2):
+        for odd in range(2):
+            for z in range(2):
+                target = peer(z * lanes + lane_of(half, odd))
+                pl.semaphore_signal(barrier, inc=1, device_id=target)
     pl.semaphore_signal(barrier, inc=1, device_id=beside)
 
     @pl.when(core == 1)
     def _():
         pl.semaphore_signal(barrier, inc=1, device_id={"tm": me, "gz": (slab + 1) % slabs})
 
-
-    def greet(step, _):
-        pl.semaphore_signal(barrier, inc=1, device_id=peer((chip + step) % chips))
-        return 0
-
-    lax.fori_loop(1, chips, greet, 0)
     def kappa_copy(side):
         return pltpu.make_async_remote_copy(
             src_ref=rim.at[side],
@@ -104,21 +117,6 @@
             )
             for field, source in enumerate((state_hbm, adjoint_hbm))
         ]
-
-    def lane_of(half, odd):
-        if lanes != 8:
-            return (chip + 2 * half + odd) % lanes
-        outer = half % 3 == 0
-        if isinstance(half, int):
-            move_x = 2 - 2 * (half // 3) if outer else 1 + 2 * odd
-            move_y = odd if outer else half - 1
-        else:
-            move_x = jnp.where(outer, 2 - 2 * (half // 3), 1 + 2 * odd)
-            move_y = jnp.where(outer, odd, half - 1)
-        return ((chip // 4 + move_y) % 2) * 4 + (chip % 4 + move_x) % 4
-
-    pairs = lanes // 2
-    classes = (pairs + 1) // 2
 
     lane = lax.broadcasted_iota(jnp.int32, (8, COL), 1)
     row = lax.broadcasted_iota(jnp.int32, (8, COL), 0)
@@ -256,39 +254,12 @@
         )
 
     def await_entry(lot, kind):
-        def take(count):
-            blocks = entry_in.at[lot, pl.ds(0, count)]
-            pltpu.make_async_copy(blocks, blocks, entry_recv.at[lot, kind]).wait()
-
-        count = 2 * lanes // classes
-        if classes == 1:
-            take(count - 1)
-        else:
-
-            @pl.when(kind == classes - 1)
-            def _():
-                take(count - 1)
-
-            @pl.when(kind < classes - 1)
-            def _():
-                take(count)
-
-    def send_carry(lot, block, odd):
-        if odd:
-            carry_copy(lot, block).start()
-        else:
-
-            @pl.when(block != chip)
-            def _():
-                carry_copy(lot, block).start()
-
-            @pl.when(block == chip)
-            def _():
-                carry_in[lot, chip] = carry_out[lot, block]
+        blocks = entry_in.at[lot, pl.ds(0, chips // classes)]
+        pltpu.make_async_copy(blocks, blocks, entry_recv.at[lot, kind]).wait()
 
     def powers(group):
         for direction in range(2):
-            factor = power[group, chip, direction]
+            factor = base[group, direction]
             run = factor
             for step in range(1, chips + 1):
                 growth[group, step, direction] = run
@@ -297,7 +268,7 @@
     def exchange(sweep, group):
         lot = sweep * groups + group
 
-        arrived = carry_in.at[lot, pl.ds(0, chips - 1)]
+        arrived = carry_in.at[lot]
         pltpu.make_async_copy(arrived, arrived, carry_recv.at[lot]).wait()
         for direction, wrap in ((0, ALPHA), (1, 1.0 / ALPHA)):
             factor = growth[group, 1, direction]
@@ -314,20 +285,11 @@
                 if step:
                     value = before[step] + start * growth[group, step, direction]
                 entry_out[lot, place, direction] = value
-        entry_in[lot, chip] = entry_out[lot, chip]
-
         for half in range(pairs):
             for odd in range(2):
                 for z in range(2):
                     other = z * lanes + lane_of(half, odd)
-                    if half == pairs - 1 or lanes != 8:
-
-                        @pl.when(other != chip)
-                        def _():
-                            entry_copy(lot, other, half // 2).start()
-
-                    else:
-                        entry_copy(lot, other, half // 2).start()
+                    entry_copy(lot, other, half // 2).start()
 
     def sums(values, forward, backward):
         ahead = values[0]
@@ -337,6 +299,14 @@
             behind = values[times - 1 - step] + backward * behind
         return ahead, behind
 
+    base_copy = pltpu.make_async_remote_copy(
+        src_ref=power.at[:, chip],
+        dst_ref=base,
+        send_sem=base_sem.at[0],
+        recv_sem=base_sem.at[1],
+        device_id=pair,
+    )
+    base_copy.start()
     gain_store = pltpu.make_async_copy(solve.at[3], gain_out.at[rows], load_sem.at[3])
     gain_give = pltpu.make_async_remote_copy(
         src_ref=solve.at[3],
@@ -365,7 +335,7 @@
                     carry_out[group, block, 1] = lead * sides[1][1] - HALF * sides[0][1]
             for odd in range(2):
                 for z in range(2):
-                    send_carry(group, z * lanes + lane_of(half, odd), odd)
+                    carry_copy(group, z * lanes + lane_of(half, odd)).start()
             return 0
 
         lax.fori_loop(0, pairs, pair_sums, 0)
@@ -376,6 +346,7 @@
         first_sums(group)
     gain_store.start()
     gain_give.start()
+    base_copy.wait_recv()
     for group in range(groups):
         powers(group)
     for group in range(groups):
@@ -534,7 +505,7 @@
                     carry_out[lot, block, 1] = lead * sides[1][1][z] - HALF * sides[0][1][z]
             for odd in (1, 0):
                 for z in range(2):
-                    send_carry(groups + group, z * lanes + lane_of(half, odd), odd)
+                    carry_copy(groups + group, z * lanes + lane_of(half, odd)).start()
             return 0
 
         lax.fori_loop(0, pairs, pair_sums, 0)
@@ -593,14 +564,15 @@
 
     gain_store.wait()
     gain_give.wait()
+    base_copy.wait_send()
 
     @pl.when(core == 1)
     def _():
         drain(rim.at[pl.ds(0, 2)], kappa_send)
 
     drain(rhs.at[:, own_times], rhs_send)
-    drain(carry_out.at[:, pl.ds(0, chips - 1)], carry_send)
-    drain(entry_out.at[:, pl.ds(0, chips - 1)], entry_send)
+    drain(carry_out, carry_send)
+    drain(entry_out, entry_send)
     drain(edge_out, edge_send)
     drain(result.at[:, own_times], give_send)
     drain(result.at[:, own_times], store_sem)
@@ -641,6 +613,7 @@
                 pltpu.VMEM((2, 3, 2, 16, cells), f32),
                 pltpu.VMEM((6, 16, cells), f32),
                 pltpu.VMEM((groups, chips, 2, 8, COL), f32),
+                pltpu.VMEM((groups, 2, 8, COL), f32),
                 pltpu.VMEM((groups, chips + 1, 2, 8, COL), f32),
                 exchanged,
                 exchanged,
@@ -654,6 +627,7 @@
                 dma,
                 dma,
                 dma((2,)),
+                dma((2,)),
                 dma,
                 dma((2 * groups,)),
                 dma,

time: 41.7 us -> 39.8 us (0.954)
  Pallas kernels: 39.4 us -> 37.4 us
    pallas_call x1, Pallas kernels: 39.4 us -> 37.4 us  [body(): both, gain = call(*held)]
where the time goes in v3:
time: 39.8 us; the launch traced here: 39.6 us
  Pallas kernels  37.4 us (94%)
  other arithmetic  1.56 us (4%)
  between operations  0.64 us (2%)
    pallas_call x1, Pallas kernels, body(): both, gain = call(*held)  37.4 us
    mul x1, other arithmetic, body(): return (both[0] * gain, both[1] * gain)  1.56 us

profile of v3, /device:TPU:1, one launch (start us, length us, event | category | flops | bytes accessed | tf_op | source)
XLA Modules:
  0.0 39.6 jit_solution(9369832842124877898)
XLA Ops:
  0.6 37.4 %shard_map.59 = (f32[2,4,32,2048]{3,2,1,0:T(8,128)S(1)}, f32[32,2048]{1,0:T(8,128)S(1)}) custom-call(f32[4,32,2048]{2,1,0:T(8,128)} %state_hbm.1, f32[4,32,2048]{2,1,0:T(8,128)} %adjoint_hbm.1, f32[32,2048]{1,0:T(8,128)} %kappa_hbm.1, f32[3,32,2048]{2,1,0:T(8,128)} %speed_hbm.1), custom_call_target="tpu_custom_call" | custom-call | flops 15728640 | bytes 5242880 | tf_op jit(solution)/shard_map/pallas_call | solution.py:652
  38.1 1.6 %bitcast_multiply_fusion = (f32[4,32,2048]{2,1,0:T(8,128)}, f32[4,32,2048]{2,1,0:T(8,128)}) fusion(f32[2,4,32,2048]{3,2,1,0:T(8,128)S(1)} %get-tuple-element.4, f32[32,2048]{1,0:T(8,128)S(1)} %get-tuple-element.5), kind=kLoop, calls=%fused_computation | loop fusion | flops 524288 | bytes 4456448 | tf_op jit(solution)/shard_map/mul | solution.py:653

commit v4 on v3

--- a/solution.py
+++ b/solution.py
@@ -24,9 +24,10 @@
     both_out, gain_out,
     rhs, first, twist, result, kappa, edge_row, rim, speed, couple, solve, power, base, growth,
     carry_out, carry_in, entry_out, entry_in, edge_out, edge_in,
+    response, entered, pack_out, pack_in, twin, given, twin_entry,
     load_sem, rhs_send, rhs_recv, kappa_send, kappa_recv, gain_sem, base_sem,
     carry_send, carry_recv, entry_send, entry_recv,
-    edge_send, edge_recv, store_sem, give_send, give_recv,
+    edge_send, edge_recv, pack_send, pack_recv, twin_send, twin_recv, twin_entry_send, twin_entry_recv, give_send, give_recv,
 ):
     half_times = times // 2
     lanes = chips // 2
@@ -316,6 +317,17 @@
         device_id=pair,
     )
 
+    twin_copies = [
+        pltpu.make_async_remote_copy(
+            src_ref=solve.at[source],
+            dst_ref=twin.at[target],
+            send_sem=twin_send,
+            recv_sem=twin_recv,
+            device_id=pair,
+        )
+        for target, source in enumerate((1, 4))
+    ]
+
     def first_sums(group):
         def pair_sums(half, _):
             for odd in range(2):
@@ -346,37 +358,32 @@
         first_sums(group)
     gain_store.start()
     gain_give.start()
+    for copy in twin_copies:
+        copy.start()
     base_copy.wait_recv()
     for group in range(groups):
         powers(group)
-    for group in range(groups):
-        exchange(0, group)
-
-    def solved(sweep, group, lane, z, emit):
+    def solved(group, lane, z, scaled, ahead, back, emit):
         here = pl.ds(pl.multiple_of(group * width + lane * COL, COL), COL)
         there = slice(z * 8, z * 8 + 8)
-        lot = sweep * groups + group
-        block = z * lanes + lane
         lead = solve[0, there, here]
         forward = solve[1, there, here]
         backward = solve[2, there, here]
         gain = solve[3, there, here]
         cross = solve[4, there, here]
         plain = solve[5, there, here]
-        back = entry_in[lot, block, 1]
         backs = [None] * times
         for j in reversed(range(times)):
             backs[j] = backward * back
             back = (
                 lead * rhs[1, j, there, here] - HALF * rhs[0, j, there, here] + backs[j]
             )
-        ahead = entry_in[lot, block, 0]
         for j in range(times):
             adjoint = rhs[1, j, there, here]
             ahead = lead * rhs[0, j, there, here] + HALF * adjoint + forward * ahead
             state = ahead + cross * backs[j]
             adjoint = backs[j] - cross * ahead + plain * adjoint
-            if sweep == 0:
+            if scaled:
                 state, adjoint = gain * state, gain * adjoint
             emit(j, state, adjoint)
 
@@ -402,11 +409,6 @@
     def first_values(group):
         def pair_values(step, _):
             half = pairs - 1 - step
-
-            @pl.when(step % 2 == 0)
-            def _():
-                await_entry(group, half // 2)
-
             for odd in (1, 0):
                 lane = lane_of(half, odd)
                 column = group * lanes + lane
@@ -423,7 +425,10 @@
                         edge_out[z, j : j + 1, here] = state[edge]
                         edge_out[z, times + j : times + j + 1, here] = adjoint[edge]
 
-                    solved(0, group, lane, z, emit)
+                    solved(group, lane, z, True, zero, zero, emit)
+                    line = z * 15
+                    edge_out[z, 2 * times : 2 * times + 1, here] = solve[1, line : line + 1, here]
+                    edge_out[z, 2 * times + 1 : 2 * times + 2, here] = solve[4, line : line + 1, here]
             for odd in (1, 0):
                 for copy in edge_copies(group * lanes + lane_of(half, odd), group * classes + half // 2):
                     copy.start()
@@ -434,15 +439,83 @@
     for group in range(groups):
         first_values(group)
 
-    def second_sums(group):
-        def pair_sums(step, _):
+    for group in range(groups):
+        exchange(0, group)
+
+    tiles = (slice(0, 8), slice(8, 16))
+
+    def column_of(column):
+        return pl.ds(pl.multiple_of((column % columns) * COL, COL), COL)
+
+    def in_z(own, below, above):
+        up = [turn(value, 1, 0) for value in own]
+        down = [turn(value, -1, 0) for value in own]
+        return (
+            [jnp.where(last_row, up[1], up[0]), jnp.where(last_row, above, up[1])],
+            [jnp.where(first_row, below, down[0]), jnp.where(first_row, down[0], down[1])],
+        )
+
+    def in_plane(own, before, after):
+        turned = turn(own, 64, 1)
+        return (
+            jnp.where(left, turned, turn(after, 64, 1)),
+            jnp.where(left, turn(before, 64, 1), turned),
+            turn(own, 1, 1),
+            turn(own, -1, 1),
+        )
+
+    def edge_rows(line, here):
+        return [jnp.broadcast_to(edge_in[side, line : line + 1, here], (8, COL)) for side in range(2)]
+
+    def make_responses(column):
+        here, before, after = column_of(column), column_of(column + columns - 1), column_of(column + 1)
+        sides = []
+        for index, line in ((1, 2 * times), (4, 2 * times + 1)):
+            own = [solve[index, there, here] for there in tiles]
+            z_ahead, z_behind = in_z(own, *edge_rows(line, here))
+            sides.append(
+                [
+                    (z_ahead[z], z_behind[z])
+                    + in_plane(own[z], solve[index, tiles[z], before], solve[index, tiles[z], after])
+                    for z in range(2)
+                ]
+            )
+        square_ratio = ratio * ratio
+        for z in range(2):
+            there = tiles[z]
+            lead = solve[0, there, here]
+            base_own = solve[1, there, here]
+            square_own = base_own * base_own
+            fourth_own = square_own * square_own
+            for place in range(6):
+                base_near, cross_near = sides[0][z][place], sides[1][z][place]
+                square_near = base_near * base_near
+                mixed = (base_own + base_near) * (square_own + square_near)
+                mixed = mixed * (fourth_own + square_near * square_near)
+                product = square_ratio * (base_own * base_near)
+                square = product * product
+                series = (1.0 + product) * (1.0 + square) * (1.0 + square * square)
+                to_state = couple[0, place // 2, place % 2, there, here]
+                to_adjoint = couple[1, place // 2, place % 2, there, here]
+                state_lead, state_half = lead * to_state, HALF * to_state
+                adjoint_lead, adjoint_half = lead * to_adjoint, HALF * to_adjoint
+                response[place, 0, there, here] = mixed * (state_lead - cross_near * adjoint_half)
+                response[place, 1, there, here] = series * (cross_near * state_lead + adjoint_half)
+                response[place, 2, there, here] = -series * (state_half + cross_near * adjoint_lead)
+                response[place, 3, there, here] = (square_ratio**7 * mixed) * (
+                    adjoint_lead - cross_near * state_half
+                )
+
+    def couplings(group, summed):
+        def pair_couplings(step, _):
             half = pairs - 1 - step
-
-            @pl.when(step % 2 == 0)
-            def _():
-                arrived = edge_in.at[:, :, pl.ds(0, 2 * pairs // classes * COL)]
-                sem = edge_recv.at[group * classes + half // 2]
-                pltpu.make_async_copy(arrived, arrived, sem).wait()
+            if summed:
+
+                @pl.when(step % 2 == 0)
+                def _():
+                    arrived = edge_in.at[:, :, pl.ds(0, 2 * pairs // classes * COL)]
+                    sem = edge_recv.at[group * classes + half // 2]
+                    pltpu.make_async_copy(arrived, arrived, sem).wait()
 
             for odd in (1, 0):
                 lane = lane_of(half, odd)
@@ -450,9 +523,7 @@
                 lane0 = column * COL
                 here = pl.ds(pl.multiple_of(lane0, COL), COL)
                 shifted = pl.ds(pl.multiple_of(lane0 + COL, COL), COL)
-                before = here
                 after = pl.ds(pl.multiple_of(lane0 + 2 * COL, COL), COL)
-                tiles = (slice(0, 8), slice(8, 16))
                 forward = [solve[1, there, here] for there in tiles]
                 backward = [solve[2, there, here] for there in tiles]
                 sides = []
@@ -466,22 +537,13 @@
                     behind_sum = [zero, zero]
                     scale = [jnp.ones((8, COL), jnp.float32)] * 2
                     for j in range(times):
-                        line = field * times + j
-                        below = jnp.broadcast_to(edge_in[0, line : line + 1, here], (8, COL))
-                        above = jnp.broadcast_to(edge_in[1, line : line + 1, here], (8, COL))
                         own = [first[field, j, there, here] for there in tiles]
-                        up = [turn(value, 1, 0) for value in own]
-                        down = [turn(value, -1, 0) for value in own]
-                        z_ahead = [jnp.where(last_row, up[1], up[0]), jnp.where(last_row, above, up[1])]
-                        z_behind = [
-                            jnp.where(first_row, below, down[0]),
-                            jnp.where(first_row, down[0], down[1]),
-                        ]
+                        z_ahead, z_behind = in_z(own, *edge_rows(field * times + j, here))
                         for z in range(2):
                             there = tiles[z]
                             turned = twist[field, j, there, shifted]
                             x_ahead = jnp.where(left, turned, twist[field, j, there, after])
-                            x_behind = jnp.where(left, twist[field, j, there, before], turned)
+                            x_behind = jnp.where(left, twist[field, j, there, here], turned)
                             value = (
                                 rhs[field, j, there, here]
                                 + weights[0][z] * z_ahead[z]
@@ -492,75 +554,292 @@
                                 + weights[5][z] * turn(own[z], -1, 1)
                             )
                             rhs[field, j, there, here] = value
-                            ahead_sum[z] = value + forward[z] * ahead_sum[z]
-                            behind_sum[z] = behind_sum[z] + scale[z] * value
-                            if j < times - 1:
-                                scale[z] = scale[z] * backward[z]
+                            if summed:
+                                ahead_sum[z] = value + forward[z] * ahead_sum[z]
+                                behind_sum[z] = behind_sum[z] + scale[z] * value
+                                if j < times - 1:
+                                    scale[z] = scale[z] * backward[z]
                     sides.append((ahead_sum, behind_sum))
+                if summed:
+                    make_responses(column)
+                    for z in range(2):
+                        lead = solve[0, tiles[z], here]
+                        block = z * lanes + lane
+                        lot = groups + group
+                        carry_out[lot, block, 0] = lead * sides[0][0][z] + HALF * sides[1][0][z]
+                        carry_out[lot, block, 1] = lead * sides[1][1][z] - HALF * sides[0][1][z]
+            return 0
+
+        lax.fori_loop(0, pairs, pair_couplings, 0)
+
+    for group in range(groups):
+        couplings(group, True)
+
+    def entries(group):
+        def pair_entries(step, _):
+            half = pairs - 1 - step
+
+            @pl.when(step % 2 == 0)
+            def _():
+                await_entry(group, half // 2)
+
+            for odd in (1, 0):
+                lane = lane_of(half, odd)
+                here = pl.ds(pl.multiple_of((group * lanes + lane) * COL, COL), COL)
                 for z in range(2):
-                    lead = solve[0, tiles[z], here]
-                    block = z * lanes + lane
-                    lot = groups + group
-                    carry_out[lot, block, 0] = lead * sides[0][0][z] + HALF * sides[1][0][z]
-                    carry_out[lot, block, 1] = lead * sides[1][1][z] - HALF * sides[0][1][z]
-            for odd in (1, 0):
+                    gain = solve[3, tiles[z], here]
+                    for index in range(2):
+                        entered[index, 8 + z * 8 : 16 + z * 8, here] = (
+                            gain * solve[1 + index, tiles[z], here] * entry_in[group, z * lanes + lane, index]
+                        )
+            return 0
+
+        lax.fori_loop(0, pairs, pair_entries, 0)
+
+    for group in range(groups):
+        entries(group)
+    for side in range(2):
+        for index in range(2):
+            for column in range(columns):
+                part = slice(column * COL, column * COL + COL)
+                line = 8 + 15 * side
+                pack_out[side, index, column : column + 1, :] = entered[index, line : line + 1, part]
+    pack_copies = [
+        pltpu.make_async_remote_copy(
+            src_ref=pack_out.at[1 - core],
+            dst_ref=pack_in.at[core],
+            send_sem=pack_send,
+            recv_sem=pack_recv.at[0],
+            device_id=pair,
+        ),
+        pltpu.make_async_remote_copy(
+            src_ref=pack_out.at[core],
+            dst_ref=pack_in.at[1 - core],
+            send_sem=pack_send,
+            recv_sem=pack_recv.at[1],
+            device_id=beside,
+        ),
+    ]
+    for copy in pack_copies:
+        copy.start()
+
+    def unpack(side):
+        for index in range(2):
+            for column in range(columns):
+                part = slice(column * COL, column * COL + COL)
+                line = 7 + 17 * side
+                entered[index, line : line + 1, part] = pack_in[side, index, column : column + 1, :]
+
+    def second_sums(step, _):
+        for k in range(4):
+            column = step * 4 + k
+            here, before, after = column_of(column), column_of(column + columns - 1), column_of(column + 1)
+            lot = groups + column // lanes
+            sides = [[], []]
+            for index in range(2):
+                own = [entered[index, 8 + z * 8 : 16 + z * 8, here] for z in range(2)]
+                z_ahead, z_behind = in_z(own, zero, zero)
                 for z in range(2):
+                    centre = slice(8 + z * 8, 16 + z * 8)
+                    sides[z].append(
+                        (z_ahead[z], z_behind[z])
+                        + in_plane(own[z], entered[index, centre, before], entered[index, centre, after])
+                    )
+            for z in range(2):
+                block = z * lanes + column % lanes
+                for direction in range(2):
+                    total_sum = carry_out[lot, block, direction]
+                    for place in range(6):
+                        for index in range(2):
+                            factor = response[place, 2 * direction + index, tiles[z], here]
+                            total_sum = total_sum + factor * sides[z][index][place]
+                    carry_out[lot, block, direction] = total_sum
+        return 0
+
+    lax.fori_loop(0, columns // 4, second_sums, 0)
+
+    def add_rows(side):
+        z, place, edge = side, 1 - side, (last_row if side else first_row)
+        for column in range(columns):
+            here = slice(column * COL, column * COL + COL)
+            lot, block = groups + column // lanes, z * lanes + column % lanes
+            enter = [
+                jnp.broadcast_to(pack_in[side, index, column : column + 1, :], (8, COL)) for index in range(2)
+            ]
+            for direction in range(2):
+                more = (
+                    response[place, 2 * direction, tiles[z], here] * enter[0]
+                    + response[place, 2 * direction + 1, tiles[z], here] * enter[1]
+                )
+                carry_out[lot, block, direction] = carry_out[lot, block, direction] + jnp.where(edge, more, 0.0)
+        for group in range(groups):
+            for half in range(pairs):
+                for odd in range(2):
                     carry_copy(groups + group, z * lanes + lane_of(half, odd)).start()
-            return 0
-
-        lax.fori_loop(0, pairs, pair_sums, 0)
-
-    for group in range(groups):
-        second_sums(group)
-    for group in range(groups):
-        exchange(1, group)
-
-    def store_copy(column):
-        part = pl.ds(pl.multiple_of(column * COL, COL), COL)
-        return pltpu.make_async_copy(
-            result.at[:, own_times, :, part], both_out.at[:, :, rows, part], store_sem
-        )
-
+
+    for outer in range(2):
+        pack_copies[outer].wait_recv()
+        for side in range(2):
+
+            @pl.when(core == (side if outer else 1 - side))
+            def _():
+                add_rows(side)
+
+    for side in range(2):
+        unpack(side)
+
+    def entered_values(step, _):
+        for k in range(2):
+            column_values(step * 2 + k)
+        return 0
+
+    def column_values(column):
+        here = pl.ds(pl.multiple_of(column * COL, COL), COL)
+        shifted = pl.ds(pl.multiple_of(column * COL + COL, COL), COL)
+
+        def emit_all(ahead, behind, forward, backward, cross, emit):
+            behinds = [behind]
+            for _ in range(times - 1):
+                behinds.append(behinds[-1] * backward)
+            for j in range(times):
+                emit(j, ahead + cross * behinds[times - 1 - j], behinds[times - 1 - j] - cross * ahead)
+                if j < times - 1:
+                    ahead = ahead * forward
+
+        for z in range(2):
+
+            def emit(j, state, adjoint):
+                first[0, j, tiles[z], here] = state
+                first[1, j, tiles[z], here] = adjoint
+                twist[0, j, tiles[z], shifted] = turn(state, 64, 1)
+                twist[1, j, tiles[z], shifted] = turn(adjoint, 64, 1)
+
+            own = slice(8 + z * 8, 16 + z * 8)
+            emit_all(
+                entered[0, own, here],
+                entered[1, own, here],
+                solve[1, tiles[z], here],
+                solve[2, tiles[z], here],
+                solve[4, tiles[z], here],
+                emit,
+            )
+        for side in range(2):
+
+            def emit(j, state, adjoint):
+                edge_in[side, j : j + 1, here] = state
+                edge_in[side, times + j : times + j + 1, here] = adjoint
+
+            line = slice(7 + 17 * side, 8 + 17 * side)
+            forward = edge_in[side, 2 * times : 2 * times + 1, here]
+            cross = edge_in[side, 2 * times + 1 : 2 * times + 2, here]
+            emit_all(
+                entered[0, line, here],
+                entered[1, line, here],
+                forward,
+                forward * (ratio * ratio),
+                cross,
+                emit,
+            )
+
+    lax.fori_loop(0, columns // 2, entered_values, 0)
     def give_copy(column):
         part = pl.ds(pl.multiple_of(column * COL, COL), COL)
         return pltpu.make_async_remote_copy(
             src_ref=result.at[:, pair_times, :, part],
-            dst_ref=both_out.at[:, :, rows, part],
+            dst_ref=given.at[:, :, :, part],
             send_sem=give_send,
             recv_sem=give_recv,
             device_id=pair,
         )
 
-    def second_values(group):
-        def pair_values(step, _):
-            half = pairs - 1 - step
-
-            @pl.when(step % 2 == 0)
-            def _():
-                await_entry(groups + group, half // 2)
-
-            for odd in (1, 0):
-                lane = lane_of(half, odd)
-                here = pl.ds(pl.multiple_of((group * lanes + lane) * COL, COL), COL)
+    def second_values(step, _):
+        for k in range(2):
+            column = step * 2 + k
+            here = pl.ds(pl.multiple_of(column * COL, COL), COL)
+            for z in range(2):
+
+                def emit(j, state, adjoint):
+                    result[0, j, tiles[z], here] = state
+                    result[1, j, tiles[z], here] = adjoint
+
+                solved(0, column, z, False, zero, zero, emit)
+        for k in range(2):
+            give_copy(step * 2 + k).start()
+        return 0
+
+    for group in range(groups):
+        couplings(group, False)
+        lax.fori_loop(group * lanes // 2, (group + 1) * lanes // 2, second_values, 0)
+        if group == groups // 2 - 1:
+            for other_group in range(groups):
+                exchange(1, other_group)
+
+    def twin_entry_copy(group):
+        return pltpu.make_async_remote_copy(
+            src_ref=entry_in.at[groups + group],
+            dst_ref=twin_entry.at[group],
+            send_sem=twin_entry_send,
+            recv_sem=twin_entry_recv,
+            device_id=pair,
+        )
+
+    for group in range(groups):
+        for kind in range(classes):
+            await_entry(groups + group, kind)
+        twin_entry_copy(group).start()
+
+    def finish(first_line, entered_at, base_at, cross_at, value_at):
+        def finish_columns(step, _):
+            for k in range(2):
+                column = step * 2 + k
+                here = pl.ds(pl.multiple_of(column * COL, COL), COL)
+                group, lane = column // lanes, column % lanes
                 for z in range(2):
-
-                    def emit(j, state, adjoint):
-                        result[0, j, z * 8 : z * 8 + 8, here] = state
-                        result[1, j, z * 8 : z * 8 + 8, here] = adjoint
-
-                    solved(1, group, lane, z, emit)
-            for odd in (1, 0):
-                give_copy(group * lanes + lane_of(half, odd)).start()
-                store_copy(group * lanes + lane_of(half, odd)).start()
+                    there = pl.ds(pl.multiple_of(first_line + z * 8, 8), 8)
+                    forward = base_at(tiles[z], here)
+                    backward = forward * (ratio * ratio)
+                    cross = cross_at(tiles[z], here)
+                    forward_half, backward_half = forward, backward
+                    for _ in range(half_times.bit_length() - 1):
+                        forward_half = forward_half * forward_half
+                        backward_half = backward_half * backward_half
+                    ahead = entered_at(group, z * lanes + lane, 0)
+                    ahead = jnp.where(core == 1, forward_half * ahead, ahead)
+                    behind = entered_at(group, z * lanes + lane, 1)
+                    behind = jnp.where(core == 1, behind, backward_half * behind)
+                    behinds = []
+                    for _ in range(half_times):
+                        behind = backward * behind
+                        behinds.append(behind)
+                    for j in range(half_times):
+                        ahead = forward * ahead
+                        behind = behinds[half_times - 1 - j]
+                        both_out[0, j, there, here] = value_at(0, j, tiles[z], here) + (ahead + cross * behind)
+                        both_out[1, j, there, here] = value_at(1, j, tiles[z], here) + (behind - cross * ahead)
             return 0
 
-        lax.fori_loop(0, pairs, pair_values, 0)
-
-    for group in range(groups):
-        second_values(group)
+        lax.fori_loop(0, columns // 2, finish_columns, 0)
 
     def drain(ref, semaphore):
         pltpu.make_async_copy(ref, ref, semaphore).wait()
+
+    finish(
+        core * 16,
+        lambda group, block, index: entry_in[groups + group, block, index],
+        lambda there, here: solve[1, there, here],
+        lambda there, here: solve[4, there, here],
+        lambda field, j, there, here: result[field, core * half_times + j, there, here],
+    )
+    drain(twin, twin_recv)
+    drain(given, give_recv)
+    drain(twin_entry, twin_entry_recv)
+    finish(
+        16 - core * 16,
+        lambda group, block, index: twin_entry[group, block, index],
+        lambda there, here: twin[0, there, here],
+        lambda there, here: twin[1, there, here],
+        lambda field, j, there, here: given[field, j, there, here],
+    )
 
     gain_store.wait()
     gain_give.wait()
@@ -574,9 +853,10 @@
     drain(carry_out, carry_send)
     drain(entry_out, entry_send)
     drain(edge_out, edge_send)
+    drain(pack_out, pack_send)
     drain(result.at[:, own_times], give_send)
-    drain(result.at[:, own_times], store_sem)
-    drain(result.at[:, own_times], give_recv)
+    drain(twin, twin_send)
+    drain(twin_entry, twin_entry_send)
 
 
 def solution(mesh):
@@ -600,7 +880,7 @@
                 pltpu.VMEM((depth, cells), f32),
             ],
             in_specs=[anywhere] * 4,
-            out_specs=[anywhere] * 2,
+            out_specs=[pl.BlockSpec(memory_space=pltpu.VMEM), anywhere],
             scratch_shapes=[
                 pltpu.VMEM((2, times, 16, cells), f32),
                 pltpu.VMEM((2, times, 16, cells), f32),
@@ -619,8 +899,15 @@
                 exchanged,
                 exchanged,
                 exchanged,
-                pltpu.VMEM((2, 2 * times, cells), f32),
-                pltpu.VMEM((2, 2 * times, cells), f32),
+                pltpu.VMEM((2, 3 * times, cells), f32),
+                pltpu.VMEM((2, 3 * times, cells), f32),
+                pltpu.VMEM((6, 4, 16, cells), f32),
+                pltpu.VMEM((2, 32, cells), f32),
+                pltpu.VMEM((2, 2, columns, COL), f32),
+                pltpu.VMEM((2, 2, columns, COL), f32),
+                pltpu.VMEM((2, 16, cells), f32),
+                pltpu.VMEM((2, steps, 16, cells), f32),
+                pltpu.VMEM((groups, chips, 2, 8, COL), f32),
                 dma((4,)),
                 dma,
                 dma((groups,)),
@@ -634,6 +921,11 @@
                 dma((2 * groups, 2)),
                 dma,
                 dma((2 * groups,)),
+                dma,
+                dma((2,)),
+                dma,
+                dma,
+                dma,
                 dma,
                 dma,
                 dma,

time: 39.8 us -> 38.1 us (0.957)
  Pallas kernels: 37.4 us -> 35.8 us
    pallas_call x1, Pallas kernels: 37.4 us -> 35.8 us  [body(): both, gain = call(*held)]
where the time goes in v4:
time: 38.1 us; the launch traced here: 38 us
  Pallas kernels  35.8 us (94%)
  other arithmetic  1.56 us (4%)
  between operations  0.64 us (2%)
    pallas_call x1, Pallas kernels, body(): both, gain = call(*held)  35.8 us
    mul x1, other arithmetic, body(): return (both[0] * gain, both[1] * gain)  1.56 us

profile of v4, /device:TPU:1, one launch (start us, length us, event | category | flops | bytes accessed | tf_op | source)
XLA Modules:
  0.0 38.0 jit_solution(8709663120345398524)
XLA Ops:
  0.6 35.8 %shard_map.59 = (f32[2,4,32,2048]{3,2,1,0:T(8,128)S(1)}, f32[32,2048]{1,0:T(8,128)S(1)}) custom-call(f32[4,32,2048]{2,1,0:T(8,128)} %state_hbm.1, f32[4,32,2048]{2,1,0:T(8,128)} %adjoint_hbm.1, f32[32,2048]{1,0:T(8,128)} %kappa_hbm.1, f32[3,32,2048]{2,1,0:T(8,128)} %speed_hbm.1), custom_call_target="tpu_custom_call" | custom-call | flops 15728640 | bytes 5242880 | tf_op jit(solution)/shard_map/pallas_call | solution.py:944
  36.4 1.6 %bitcast_multiply_fusion = (f32[4,32,2048]{2,1,0:T(8,128)}, f32[4,32,2048]{2,1,0:T(8,128)}) fusion(f32[2,4,32,2048]{3,2,1,0:T(8,128)S(1)} %get-tuple-element.4, f32[32,2048]{1,0:T(8,128)S(1)} %get-tuple-element.5), kind=kLoop, calls=%fused_computation | loop fusion | flops 524288 | bytes 4456448 | tf_op jit(solution)/shard_map/mul | solution.py:945

commit v5 on v4

--- a/solution.py
+++ b/solution.py
@@ -72,6 +72,18 @@
     def tile8(start):
         return pl.ds(pl.multiple_of(start, 8), 8)
 
+    barrier = pltpu.get_barrier_semaphore()
+    for half in range(lanes // 2):
+        for odd in range(2):
+            for z in range(2):
+                target = peer(z * lanes + lane_of(half, odd))
+                pl.semaphore_signal(barrier, inc=1, device_id=target)
+    pl.semaphore_signal(barrier, inc=1, device_id=beside)
+
+    @pl.when(core == 1)
+    def _():
+        pl.semaphore_signal(barrier, inc=1, device_id={"tm": me, "gz": (slab + 1) % slabs})
+
     loads = [
         pltpu.make_async_copy(kappa_hbm.at[rows], kappa.at[pl.ds(8, 16)], load_sem.at[0]),
         pltpu.make_async_copy(
@@ -84,18 +96,6 @@
     ]
     for load in loads:
         load.start()
-
-    barrier = pltpu.get_barrier_semaphore()
-    for half in range(lanes // 2):
-        for odd in range(2):
-            for z in range(2):
-                target = peer(z * lanes + lane_of(half, odd))
-                pl.semaphore_signal(barrier, inc=1, device_id=target)
-    pl.semaphore_signal(barrier, inc=1, device_id=beside)
-
-    @pl.when(core == 1)
-    def _():
-        pl.semaphore_signal(barrier, inc=1, device_id={"tm": me, "gz": (slab + 1) % slabs})
 
     def kappa_copy(side):
         return pltpu.make_async_remote_copy(
@@ -212,7 +212,6 @@
             coefficients(step * 4 + k, core)
         return 0
 
-    lax.fori_loop(0, cells // COL // 4, inner_coefficients, 0)
     pl.semaphore_wait(barrier, chips + 1 + core)
 
     @pl.when(core == 1)
@@ -224,6 +223,7 @@
         for copy in rhs_copies(group):
             copy.start()
 
+    lax.fori_loop(0, cells // COL // 4, inner_coefficients, 0)
     pltpu.make_async_copy(rhs.at[:, own_times], rhs.at[:, own_times], load_sem.at[2]).wait()
     kappa_copy(1).wait_recv()
     for side in range(2):
@@ -579,10 +579,6 @@
         def pair_entries(step, _):
             half = pairs - 1 - step
 
-            @pl.when(step % 2 == 0)
-            def _():
-                await_entry(group, half // 2)
-
             for odd in (1, 0):
                 lane = lane_of(half, odd)
                 here = pl.ds(pl.multiple_of((group * lanes + lane) * COL, COL), COL)
@@ -597,13 +593,18 @@
         lax.fori_loop(0, pairs, pair_entries, 0)
 
     for group in range(groups):
-        entries(group)
-    for side in range(2):
-        for index in range(2):
-            for column in range(columns):
-                part = slice(column * COL, column * COL + COL)
-                line = 8 + 15 * side
-                pack_out[side, index, column : column + 1, :] = entered[index, line : line + 1, part]
+        for kind in range(classes):
+            await_entry(group, kind)
+        for lane in range(lanes):
+            column = group * lanes + lane
+            here = slice(column * COL, column * COL + COL)
+            for side in range(2):
+                line, edge, block = slice(15 * side, 15 * side + 1), slice(7 * side, 7 * side + 1), side * lanes + lane
+                gain = solve[3, line, here]
+                for index in range(2):
+                    pack_out[side, index, column : column + 1, :] = (
+                        gain * solve[1 + index, line, here] * entry_in[group, block, index, edge]
+                    )
     pack_copies = [
         pltpu.make_async_remote_copy(
             src_ref=pack_out.at[1 - core],
@@ -622,6 +623,8 @@
     ]
     for copy in pack_copies:
         copy.start()
+    for group in range(groups):
+        entries(group)
 
     def unpack(side):
         for index in range(2):
@@ -779,21 +782,15 @@
             src_ref=entry_in.at[groups + group],
             dst_ref=twin_entry.at[group],
             send_sem=twin_entry_send,
-            recv_sem=twin_entry_recv,
+            recv_sem=twin_entry_recv.at[group],
             device_id=pair,
         )
 
-    for group in range(groups):
-        for kind in range(classes):
-            await_entry(groups + group, kind)
-        twin_entry_copy(group).start()
-
-    def finish(first_line, entered_at, base_at, cross_at, value_at):
+    def finish(group, first_line, entered_at, base_at, cross_at, value_at):
         def finish_columns(step, _):
             for k in range(2):
-                column = step * 2 + k
-                here = pl.ds(pl.multiple_of(column * COL, COL), COL)
-                group, lane = column // lanes, column % lanes
+                lane = step * 2 + k
+                here = pl.ds(pl.multiple_of((group * lanes + lane) * COL, COL), COL)
                 for z in range(2):
                     there = pl.ds(pl.multiple_of(first_line + z * 8, 8), 8)
                     forward = base_at(tiles[z], here)
@@ -803,9 +800,9 @@
                     for _ in range(half_times.bit_length() - 1):
                         forward_half = forward_half * forward_half
                         backward_half = backward_half * backward_half
-                    ahead = entered_at(group, z * lanes + lane, 0)
+                    ahead = entered_at(z * lanes + lane, 0)
                     ahead = jnp.where(core == 1, forward_half * ahead, ahead)
-                    behind = entered_at(group, z * lanes + lane, 1)
+                    behind = entered_at(z * lanes + lane, 1)
                     behind = jnp.where(core == 1, behind, backward_half * behind)
                     behinds = []
                     for _ in range(half_times):
@@ -818,28 +815,35 @@
                         both_out[1, j, there, here] = value_at(1, j, tiles[z], here) + (behind - cross * ahead)
             return 0
 
-        lax.fori_loop(0, columns // 2, finish_columns, 0)
+        lax.fori_loop(0, lanes // 2, finish_columns, 0)
 
     def drain(ref, semaphore):
         pltpu.make_async_copy(ref, ref, semaphore).wait()
 
-    finish(
-        core * 16,
-        lambda group, block, index: entry_in[groups + group, block, index],
-        lambda there, here: solve[1, there, here],
-        lambda there, here: solve[4, there, here],
-        lambda field, j, there, here: result[field, core * half_times + j, there, here],
-    )
+    for group in range(groups):
+        for kind in range(classes):
+            await_entry(groups + group, kind)
+        twin_entry_copy(group).start()
+        finish(
+            group,
+            core * 16,
+            lambda block, index: entry_in[groups + group, block, index],
+            lambda there, here: solve[1, there, here],
+            lambda there, here: solve[4, there, here],
+            lambda field, j, there, here: result[field, core * half_times + j, there, here],
+        )
     drain(twin, twin_recv)
     drain(given, give_recv)
-    drain(twin_entry, twin_entry_recv)
-    finish(
-        16 - core * 16,
-        lambda group, block, index: twin_entry[group, block, index],
-        lambda there, here: twin[0, there, here],
-        lambda there, here: twin[1, there, here],
-        lambda field, j, there, here: given[field, j, there, here],
-    )
+    for group in range(groups):
+        drain(twin_entry.at[group], twin_entry_recv.at[group])
+        finish(
+            group,
+            16 - core * 16,
+            lambda block, index: twin_entry[group, block, index],
+            lambda there, here: twin[0, there, here],
+            lambda there, here: twin[1, there, here],
+            lambda field, j, there, here: given[field, j, there, here],
+        )
 
     gain_store.wait()
     gain_give.wait()
@@ -857,6 +861,15 @@
     drain(result.at[:, own_times], give_send)
     drain(twin, twin_send)
     drain(twin_entry, twin_entry_send)
+
+
+def write_kernel(both, gain, state_out, adjoint_out, stage, semaphore):
+    for field, target in enumerate((state_out, adjoint_out)):
+        for step in range(both.shape[1]):
+            stage[field, step] = both[field, step] * gain[...]
+            pltpu.make_async_copy(stage.at[field, step], target.at[step], semaphore.at[field]).start()
+    for field, target in enumerate((state_out, adjoint_out)):
+        pltpu.make_async_copy(stage.at[field], target, semaphore.at[field]).wait()
 
 
 def solution(mesh):
@@ -926,7 +939,7 @@
                 dma,
                 dma,
                 dma,
-                dma,
+                dma((groups,)),
                 dma,
                 dma,
             ],
@@ -942,7 +955,16 @@
             for array in (state_rhs, adjoint_rhs, diffusivity, velocity)
         ]
         both, gain = call(*held)
-        return both[0] * gain, both[1] * gain
+        write = pl.pallas_call(
+            write_kernel,
+            out_shape=[jax.ShapeDtypeStruct(state_rhs.shape, f32)] * 2,
+            in_specs=[pl.BlockSpec(memory_space=pltpu.VMEM)] * 2,
+            out_specs=[anywhere] * 2,
+            scratch_shapes=[pltpu.VMEM((2, steps, depth, cells), f32), dma((2,))],
+            compiler_params=pltpu.CompilerParams(vmem_limit_bytes=48 * 1024 * 1024),
+        )
+        placed_inputs = [pltpu.with_memory_space_constraint(array, pltpu.VMEM) for array in (both, gain)]
+        return tuple(write(*placed_inputs))
 
     placed = (P("tm", "gz", None), P("tm", "gz", None), P("gz", None), P(None, "gz", None))
     return jax.shard_map(

time: 38.1 us -> 37.8 us (level)
  other arithmetic: 1.56 us -> 0 us
  Pallas kernels: 35.8 us -> 37 us
    mul x1 -> x0, other arithmetic: 1.56 us -> none  [body(): return (both[0] * gain, both[1] * gain)]
    pallas_call x0 -> x1, Pallas kernels: none -> 1.35 us  [body(): return tuple(write(*placed_inputs))]
where the time goes in v5:
time: 37.8 us; the launch traced here: 37.6 us
  Pallas kernels  37 us (98%)
  between operations  0.64 us (2%)
    pallas_call x1, Pallas kernels, body(): both, gain = call(*held)  35.6 us
    pallas_call x1, Pallas kernels, body(): return tuple(write(*placed_inputs))  1.35 us

profile of v5, /device:TPU:1, one launch (start us, length us, event | category | flops | bytes accessed | tf_op | source)
XLA Modules:
  0.0 37.6 jit_solution(15709354959098501594)
XLA Ops:
  0.6 35.6 %shard_map.59 = (f32[2,4,32,2048]{3,2,1,0:T(8,128)S(1)}, f32[32,2048]{1,0:T(8,128)S(1)}) custom-call(f32[4,32,2048]{2,1,0:T(8,128)} %state_hbm.1, f32[4,32,2048]{2,1,0:T(8,128)} %adjoint_hbm.1, f32[32,2048]{1,0:T(8,128)} %kappa_hbm.1, f32[3,32,2048]{2,1,0:T(8,128)} %speed_hbm.1), custom_call_target="tpu_custom_call" | custom-call | flops 15728640 | bytes 5242880 | tf_op jit(solution)/shard_map/pallas_call | solution.py:957
  36.3 1.4 %shard_map.60 = (f32[4,32,2048]{2,1,0:T(8,128)}, f32[4,32,2048]{2,1,0:T(8,128)}) custom-call(f32[2,4,32,2048]{3,2,1,0:T(8,128)S(1)} %get-tuple-element.4.both, f32[32,2048]{1,0:T(8,128)S(1)} %get-tuple-element.5.gain), custom_call_target="tpu_custom_call" | custom-call | tf_op jit(solution)/shard_map/pallas_call | solution.py:967

commit v6 on v5

--- a/solution.py
+++ b/solution.py
@@ -208,8 +208,8 @@
         return 0
 
     def outer_coefficients(step, _):
-        for k in range(4):
-            coefficients(step * 4 + k, core)
+        for k in range(8):
+            coefficients(step * 8 + k, core)
         return 0
 
     pl.semaphore_wait(barrier, chips + 1 + core)
@@ -234,7 +234,7 @@
                 part = slice(piece * piece_width, piece * piece_width + piece_width)
                 kappa[7 + 17 * side : 8 + 17 * side, part] = rim[2, piece : piece + 1, :]
 
-    lax.fori_loop(0, cells // COL // 4, outer_coefficients, 0)
+    lax.fori_loop(0, cells // COL // 8, outer_coefficients, 0)
 
     def carry_copy(lot, other):
         return pltpu.make_async_remote_copy(
@@ -329,8 +329,9 @@
     ]
 
     def first_sums(group):
-        def pair_sums(half, _):
-            for odd in range(2):
+        def quad_sums(step, _):
+            places = [(2 * step + more, odd) for more in range(2) for odd in range(2)]
+            for half, odd in places:
                 lane = lane_of(half, odd)
                 here = pl.ds(pl.multiple_of(group * width + lane * COL, COL), COL)
                 for z in range(2):
@@ -345,12 +346,12 @@
                     block = z * lanes + lane
                     carry_out[group, block, 0] = lead * sides[0][0] + HALF * sides[1][0]
                     carry_out[group, block, 1] = lead * sides[1][1] - HALF * sides[0][1]
-            for odd in range(2):
+            for half, odd in places:
                 for z in range(2):
                     carry_copy(group, z * lanes + lane_of(half, odd)).start()
             return 0
 
-        lax.fori_loop(0, pairs, pair_sums, 0)
+        lax.fori_loop(0, pairs // 2, quad_sums, 0)
 
     for group in range(groups):
         arrived = rhs.at[:, own_times, :, slice(0, width)]
@@ -788,8 +789,8 @@
 
     def finish(group, first_line, entered_at, base_at, cross_at, value_at):
         def finish_columns(step, _):
-            for k in range(2):
-                lane = step * 2 + k
+            for k in range(4):
+                lane = step * 4 + k
                 here = pl.ds(pl.multiple_of((group * lanes + lane) * COL, COL), COL)
                 for z in range(2):
                     there = pl.ds(pl.multiple_of(first_line + z * 8, 8), 8)
@@ -815,7 +816,7 @@
                         both_out[1, j, there, here] = value_at(1, j, tiles[z], here) + (behind - cross * ahead)
             return 0
 
-        lax.fori_loop(0, lanes // 2, finish_columns, 0)
+        lax.fori_loop(0, lanes // 4, finish_columns, 0)
 
     def drain(ref, semaphore):
         pltpu.make_async_copy(ref, ref, semaphore).wait()

time: 37.8 us -> 37.7 us (level)
  no operation moved by 1% of the time
where the time goes in v6:
time: 37.7 us; the launch traced here: 37.5 us
  Pallas kernels  36.9 us (98%)
  between operations  0.64 us (2%)
    pallas_call x1, Pallas kernels, body(): both, gain = call(*held)  35.6 us
    pallas_call x1, Pallas kernels, body(): return tuple(write(*placed_inputs))  1.35 us

profile of v6, /device:TPU:1, one launch (start us, length us, event | category | flops | bytes accessed | tf_op | source)
XLA Modules:
  0.0 37.5 jit_solution(13705140349174906386)
XLA Ops:
  0.6 35.6 %shard_map.59 = (f32[2,4,32,2048]{3,2,1,0:T(8,128)S(1)}, f32[32,2048]{1,0:T(8,128)S(1)}) custom-call(f32[4,32,2048]{2,1,0:T(8,128)} %state_hbm.1, f32[4,32,2048]{2,1,0:T(8,128)} %adjoint_hbm.1, f32[32,2048]{1,0:T(8,128)} %kappa_hbm.1, f32[3,32,2048]{2,1,0:T(8,128)} %speed_hbm.1), custom_call_target="tpu_custom_call" | custom-call | flops 15728640 | bytes 5242880 | tf_op jit(solution)/shard_map/pallas_call | solution.py:958
  36.2 1.4 %shard_map.60 = (f32[4,32,2048]{2,1,0:T(8,128)}, f32[4,32,2048]{2,1,0:T(8,128)}) custom-call(f32[2,4,32,2048]{3,2,1,0:T(8,128)S(1)} %get-tuple-element.4.both, f32[32,2048]{1,0:T(8,128)S(1)} %get-tuple-element.5.gain), custom_call_target="tpu_custom_call" | custom-call | tf_op jit(solution)/shard_map/pallas_call | solution.py:968

commit v7 on v6

--- a/solution.py
+++ b/solution.py
@@ -21,11 +21,11 @@
 def kernel(
     chips, slabs, cells, times,
     state_hbm, adjoint_hbm, kappa_hbm, speed_hbm,
-    both_out, gain_out,
+    both_out,
     rhs, first, twist, result, kappa, edge_row, rim, speed, couple, solve, power, base, growth,
     carry_out, carry_in, entry_out, entry_in, edge_out, edge_in,
     response, entered, pack_out, pack_in, twin, given, twin_entry,
-    load_sem, rhs_send, rhs_recv, kappa_send, kappa_recv, gain_sem, base_sem,
+    load_sem, rhs_send, rhs_recv, kappa_send, kappa_recv, base_sem,
     carry_send, carry_recv, entry_send, entry_recv,
     edge_send, edge_recv, pack_send, pack_recv, twin_send, twin_recv, twin_entry_send, twin_entry_recv, give_send, give_recv,
 ):
@@ -308,15 +308,6 @@
         device_id=pair,
     )
     base_copy.start()
-    gain_store = pltpu.make_async_copy(solve.at[3], gain_out.at[rows], load_sem.at[3])
-    gain_give = pltpu.make_async_remote_copy(
-        src_ref=solve.at[3],
-        dst_ref=gain_out.at[rows],
-        send_sem=gain_sem.at[0],
-        recv_sem=gain_sem.at[1],
-        device_id=pair,
-    )
-
     twin_copies = [
         pltpu.make_async_remote_copy(
             src_ref=solve.at[source],
@@ -325,7 +316,7 @@
             recv_sem=twin_recv,
             device_id=pair,
         )
-        for target, source in enumerate((1, 4))
+        for target, source in enumerate((1, 4, 3))
     ]
 
     def first_sums(group):
@@ -357,8 +348,6 @@
         arrived = rhs.at[:, own_times, :, slice(0, width)]
         pltpu.make_async_copy(arrived, arrived, rhs_recv.at[group]).wait()
         first_sums(group)
-    gain_store.start()
-    gain_give.start()
     for copy in twin_copies:
         copy.start()
     base_copy.wait_recv()
@@ -787,7 +776,7 @@
             device_id=pair,
         )
 
-    def finish(group, first_line, entered_at, base_at, cross_at, value_at):
+    def finish(group, first_line, entered_at, base_at, cross_at, gain_at, value_at):
         def finish_columns(step, _):
             for k in range(4):
                 lane = step * 4 + k
@@ -797,6 +786,7 @@
                     forward = base_at(tiles[z], here)
                     backward = forward * (ratio * ratio)
                     cross = cross_at(tiles[z], here)
+                    gain = gain_at(tiles[z], here)
                     forward_half, backward_half = forward, backward
                     for _ in range(half_times.bit_length() - 1):
                         forward_half = forward_half * forward_half
@@ -812,8 +802,8 @@
                     for j in range(half_times):
                         ahead = forward * ahead
                         behind = behinds[half_times - 1 - j]
-                        both_out[0, j, there, here] = value_at(0, j, tiles[z], here) + (ahead + cross * behind)
-                        both_out[1, j, there, here] = value_at(1, j, tiles[z], here) + (behind - cross * ahead)
+                        both_out[0, j, there, here] = gain * (value_at(0, j, tiles[z], here) + (ahead + cross * behind))
+                        both_out[1, j, there, here] = gain * (value_at(1, j, tiles[z], here) + (behind - cross * ahead))
             return 0
 
         lax.fori_loop(0, lanes // 4, finish_columns, 0)
@@ -831,6 +821,7 @@
             lambda block, index: entry_in[groups + group, block, index],
             lambda there, here: solve[1, there, here],
             lambda there, here: solve[4, there, here],
+            lambda there, here: solve[3, there, here],
             lambda field, j, there, here: result[field, core * half_times + j, there, here],
         )
     drain(twin, twin_recv)
@@ -843,11 +834,10 @@
             lambda block, index: twin_entry[group, block, index],
             lambda there, here: twin[0, there, here],
             lambda there, here: twin[1, there, here],
+            lambda there, here: twin[2, there, here],
             lambda field, j, there, here: given[field, j, there, here],
         )
 
-    gain_store.wait()
-    gain_give.wait()
     base_copy.wait_send()
 
     @pl.when(core == 1)
@@ -864,13 +854,15 @@
     drain(twin_entry, twin_entry_send)
 
 
-def write_kernel(both, gain, state_out, adjoint_out, stage, semaphore):
-    for field, target in enumerate((state_out, adjoint_out)):
-        for step in range(both.shape[1]):
-            stage[field, step] = both[field, step] * gain[...]
-            pltpu.make_async_copy(stage.at[field, step], target.at[step], semaphore.at[field]).start()
-    for field, target in enumerate((state_out, adjoint_out)):
-        pltpu.make_async_copy(stage.at[field], target, semaphore.at[field]).wait()
+def write_kernel(both, state_out, adjoint_out, semaphore):
+    copies = [
+        pltpu.make_async_copy(both.at[field], target, semaphore.at[field])
+        for field, target in enumerate((state_out, adjoint_out))
+    ]
+    for copy in copies:
+        copy.start()
+    for copy in copies:
+        copy.wait()
 
 
 def solution(mesh):
@@ -889,12 +881,9 @@
         exchanged = pltpu.VMEM((2 * groups, chips, 2, 8, COL), f32)
         call = pl.pallas_call(
             functools.partial(kernel, chips, slabs, cells, times),
-            out_shape=[
-                pltpu.VMEM((2, steps, depth, cells), f32),
-                pltpu.VMEM((depth, cells), f32),
-            ],
+            out_shape=pltpu.VMEM((2, steps, depth, cells), f32),
             in_specs=[anywhere] * 4,
-            out_specs=[pl.BlockSpec(memory_space=pltpu.VMEM), anywhere],
+            out_specs=pl.BlockSpec(memory_space=pltpu.VMEM),
             scratch_shapes=[
                 pltpu.VMEM((2, times, 16, cells), f32),
                 pltpu.VMEM((2, times, 16, cells), f32),
@@ -919,15 +908,14 @@
                 pltpu.VMEM((2, 32, cells), f32),
                 pltpu.VMEM((2, 2, columns, COL), f32),
                 pltpu.VMEM((2, 2, columns, COL), f32),
-                pltpu.VMEM((2, 16, cells), f32),
+                pltpu.VMEM((3, 16, cells), f32),
                 pltpu.VMEM((2, steps, 16, cells), f32),
                 pltpu.VMEM((groups, chips, 2, 8, COL), f32),
-                dma((4,)),
+                dma((3,)),
                 dma,
                 dma((groups,)),
                 dma,
                 dma,
-                dma((2,)),
                 dma((2,)),
                 dma,
                 dma((2 * groups,)),
@@ -955,17 +943,16 @@
             pltpu.with_memory_space_constraint(array, pltpu.HBM)
             for array in (state_rhs, adjoint_rhs, diffusivity, velocity)
         ]
-        both, gain = call(*held)
+        both = call(*held)
         write = pl.pallas_call(
             write_kernel,
             out_shape=[jax.ShapeDtypeStruct(state_rhs.shape, f32)] * 2,
-            in_specs=[pl.BlockSpec(memory_space=pltpu.VMEM)] * 2,
+            in_specs=[pl.BlockSpec(memory_space=pltpu.VMEM)],
             out_specs=[anywhere] * 2,
-            scratch_shapes=[pltpu.VMEM((2, steps, depth, cells), f32), dma((2,))],
+            scratch_shapes=[dma((2,))],
             compiler_params=pltpu.CompilerParams(vmem_limit_bytes=48 * 1024 * 1024),
         )
-        placed_inputs = [pltpu.with_memory_space_constraint(array, pltpu.VMEM) for array in (both, gain)]
-        return tuple(write(*placed_inputs))
+        return tuple(write(pltpu.with_memory_space_constraint(both, pltpu.VMEM)))
 
     placed = (P("tm", "gz", None), P("tm", "gz", None), P("gz", None), P(None, "gz", None))
     return jax.shard_map(

time: 37.7 us -> 37.6 us (level)
  no operation moved by 1% of the time
where the time goes in v7:
time: 37.6 us; the launch traced here: 37.5 us
  Pallas kernels  36.8 us (98%)
  between operations  0.64 us (2%)
    pallas_call x1, Pallas kernels, body(): both = call(*held)  35.5 us
    pallas_call x1, Pallas kernels, body(): return tuple(write(pltpu.with_memory_space_constraint(both, pltpu.VMEM)))  1.33 us

profile of v7, /device:TPU:1, one launch (start us, length us, event | category | flops | bytes accessed | tf_op | source)
XLA Modules:
  0.0 37.5 jit_solution(1155918803116556817)
XLA Ops:
  0.6 35.5 %shard_map.59.both = f32[2,4,32,2048]{3,2,1,0:T(8,128)S(1)} custom-call(f32[4,32,2048]{2,1,0:T(8,128)} %state_hbm.1, f32[4,32,2048]{2,1,0:T(8,128)} %adjoint_hbm.1, f32[32,2048]{1,0:T(8,128)} %kappa_hbm.1, f32[3,32,2048]{2,1,0:T(8,128)} %speed_hbm.1), custom_call_target="tpu_custom_call" | custom-call | flops 15728640 | bytes 5242880 | tf_op jit(solution)/shard_map/pallas_call | solution.py:946
  36.1 1.3 %shard_map.60 = (f32[4,32,2048]{2,1,0:T(8,128)}, f32[4,32,2048]{2,1,0:T(8,128)}) custom-call(f32[2,4,32,2048]{3,2,1,0:T(8,128)S(1)} %shard_map.59.both), custom_call_target="tpu_custom_call" | custom-call | tf_op jit(solution)/shard_map/pallas_call | solution.py:955

commit v8 on v7

--- a/solution.py
+++ b/solution.py
@@ -611,7 +611,7 @@
             device_id=beside,
         ),
     ]
-    for copy in pack_copies:
+    for copy in reversed(pack_copies):
         copy.start()
     for group in range(groups):
         entries(group)

time: 37.6 us -> 37.6 us (level)
  no operation moved by 1% of the time
where the time goes in v8:
time: 37.6 us; the launch traced here: 37.5 us
  Pallas kernels  36.8 us (98%)
  between operations  0.64 us (2%)
    pallas_call x1, Pallas kernels, body(): both = call(*held)  35.5 us
    pallas_call x1, Pallas kernels, body(): return tuple(write(pltpu.with_memory_space_constraint(both, pltpu.VMEM)))  1.33 us

profile of v8, /device:TPU:1, one launch (start us, length us, event | category | flops | bytes accessed | tf_op | source)
XLA Modules:
  0.0 37.5 jit_solution(2084650002885610760)
XLA Ops:
  0.6 35.5 %shard_map.59.both = f32[2,4,32,2048]{3,2,1,0:T(8,128)S(1)} custom-call(f32[4,32,2048]{2,1,0:T(8,128)} %state_hbm.1, f32[4,32,2048]{2,1,0:T(8,128)} %adjoint_hbm.1, f32[32,2048]{1,0:T(8,128)} %kappa_hbm.1, f32[3,32,2048]{2,1,0:T(8,128)} %speed_hbm.1), custom_call_target="tpu_custom_call" | custom-call | flops 15728640 | bytes 5242880 | tf_op jit(solution)/shard_map/pallas_call | solution.py:946
  36.1 1.3 %shard_map.60 = (f32[4,32,2048]{2,1,0:T(8,128)}, f32[4,32,2048]{2,1,0:T(8,128)}) custom-call(f32[2,4,32,2048]{3,2,1,0:T(8,128)S(1)} %shard_map.59.both), custom_call_target="tpu_custom_call" | custom-call | tf_op jit(solution)/shard_map/pallas_call | solution.py:955
